TPU v7x, 32 devices: a whole 2x2x4 slice. The times are simulated.
32 devices in a mesh: seq: 4 (over z), win: 4 (over y, x), wout: 2 (over core).
Axes of the slice: x: 2, y: 2, z: 4, core: 2. Of those that a mesh axis runs over, the one named last changes fastest.
Arguments:
- qkv_in: bfloat16 [1024, 3, 2048], P('seq', None, ('win', 'wout')), may hold values from -6 to 6
- conv_w: float32 [3, 4, 2048], P(None, None, ('win', 'wout')), may hold values from -3 to 3
- beta_logits: float32 [16, 1024], P(('win', 'wout'), 'seq'), may hold values from -10 to 3
- lengths: int32 [4], replicated, may hold values from 1 to 384, as said below
- out_gain: float32 [128], replicated, may hold values from 0.1 to 1.9
- w_out: bfloat16 [2048, 2048], P(('win', 'wout')), may hold values from -0.125 to 0.125
- hidden_in: bfloat16 [1024, 2048], P(('seq', 'win', 'wout')), may hold values from -6 to 6
- norm_gain: float32 [2048], replicated, may hold values from 0.1 to 1.9
- w_qkv: bfloat16 [2048, 6144], P('win', 'wout'), may hold values from -0.125 to 0.125
Outputs:
- qkv_next: bfloat16 [1024, 6144], P(('seq', 'win'), 'wout')
- stream_out: bfloat16 [1024, 2048], P(('seq', 'win', 'wout'))
- final_states: float32 [4, 16, 128, 128], P(None, ('win', 'wout'))
- conv_edges: bfloat16 [4, 3, 3, 2048], P(None, None, None, ('win', 'wout'))
Inputs may be any that keep to these rules, and one draw needn't show every extreme that they name: The lengths sum to 1024; the largest is exactly 384.
All inputs are finite; a program needn't handle non-finite values.
Results may differ from a plain program's by a relative error of at most 0.022.
Values may be sent and summed in bfloat16 or wider, within the bound.
A program may use at most 64 MiB of HBM per device.

v0:
```python
import jax
import jax.numpy as jnp
from jax import lax
from jax.sharding import PartitionSpec as P

DK = 128
CONV = 4
SPAN = 64
REQS = 4


def from_behind(value, axis, steps):
    count = lax.axis_size(axis)
    leading, last = (max(0, -steps), min(count, count - steps))
    return lax.ppermute(value, axis, [(source, source + steps) for source in range(leading, last)])


def segment_ids(positions, seg_ends):
    counts = jnp.sum((positions[:, None] >= seg_ends[None, :]).astype(jnp.int32), axis=1)
    return jnp.where(positions < 0, -1, counts)


def unit_rows(values):
    return values / jnp.sqrt(jnp.sum(values * values, axis=-1, keepdims=True) + 1e-06)


def outer_product(form, left, right):
    return jnp.einsum(form, left, right, precision=lax.Precision.HIGHEST)


def body(qkv_in, conv_w, beta_logits, lengths, out_gain, w_out, hidden_in, norm_gain, w_qkv):
    row_count = qkv_in.shape[0]
    local_width = qkv_in.shape[2]
    head_count = local_width // DK
    rim_rows = CONV - 1
    first_position = lax.axis_index("seq") * row_count
    seg_ends = jnp.cumsum(lengths)
    preceding_entries = from_behind(qkv_in[row_count - rim_rows :], "seq", 1)
    extended = jnp.concatenate([preceding_entries, qkv_in], axis=0)
    ext_pos = first_position - rim_rows + jnp.arange(row_count + rim_rows, dtype=jnp.int32)
    ext_seg = segment_ids(ext_pos, seg_ends)
    own_seg = ext_seg[rim_rows:]
    pre = jnp.zeros((row_count, 3, local_width), jnp.float32)
    for offset in range(CONV):
        same_request = (ext_seg[offset : offset + row_count] == own_seg).astype(jnp.float32)
        window = extended[offset : offset + row_count].astype(jnp.float32)
        pre = pre + conv_w[:, offset, :][None] * window * same_request[:, None, None]
    activated = jax.nn.silu(pre).astype(jnp.bfloat16)
    span_count = row_count // SPAN

    def blocks(values):
        return values.reshape(span_count, SPAN, head_count, DK).transpose(0, 2, 1, 3)

    query = blocks(
        unit_rows(activated[:, 0].astype(jnp.float32).reshape(row_count, head_count, DK))
    )
    keys_b = blocks(
        unit_rows(activated[:, 1].astype(jnp.float32).reshape(row_count, head_count, DK))
    )
    values_b = blocks(activated[:, 2].astype(jnp.float32).reshape(row_count, head_count, DK))
    beta_coefficient = (
        jax.nn.sigmoid(beta_logits).reshape(head_count, span_count, SPAN).transpose(1, 0, 2)
    )
    seg_blocks = own_seg.reshape(span_count, SPAN)
    before_seg = segment_ids(
        first_position + jnp.arange(span_count, dtype=jnp.int32) * SPAN - 1, seg_ends
    )
    coupled_entries = (seg_blocks == before_seg[:, None]).astype(jnp.float32)
    same = seg_blocks[:, :, None] == seg_blocks[:, None, :]
    row_ids = jnp.arange(SPAN)[:, None]
    col_ids = jnp.arange(SPAN)[None, :]
    strict = (same & (row_ids > col_ids)).astype(jnp.float32)
    causal = (same & (row_ids >= col_ids)).astype(jnp.float32)
    gram = outer_product("nhik,nhjk->nhij", keys_b, keys_b)
    system = (
        jnp.eye(SPAN, dtype=jnp.float32) + beta_coefficient[..., :, None] * gram * strict[:, None]
    )
    targets = jnp.concatenate(
        [
            beta_coefficient[..., None] * values_b,
            (beta_coefficient * coupled_entries[:, None])[..., None] * keys_b,
        ],
        axis=-1,
    )
    solved = lax.linalg.triangular_solve(
        system, targets, left_side=True, lower=True, unit_diagonal=True
    )
    u_local = solved[..., :DK]
    w_link = solved[..., DK:]
    scores = outer_product("nhik,nhjk->nhij", query, keys_b) * causal[:, None]
    out_local = outer_product("nhij,nhjv->nhiv", scores, u_local)
    query_link = coupled_entries[:, None, :, None] * query - outer_product(
        "nhij,nhjk->nhik", scores, w_link
    )
    eye_keys = jnp.eye(DK, dtype=jnp.float32)
    last_link = coupled_entries[:, -1]
    in_last = (seg_blocks == seg_blocks[:, -1:]).astype(jnp.float32)
    trans = last_link[:, None, None, None] * (
        eye_keys - outer_product("nhjk,nhjl->nhkl", keys_b, w_link)
    )
    write = outer_product("nhjk,nhjv->nhkv", keys_b * in_last[:, None, :, None], u_local)

    def fold_span(carried_state, state_pair):
        return (
            (
                outer_product("hkl,hlm->hkm", state_pair[0], carried_state[0]),
                outer_product("eat,eto->eao", state_pair[0], carried_state[1]) + state_pair[1],
            ),
            None,
        )

    identity_maps = (
        jnp.broadcast_to(eye_keys, (head_count, DK, DK)),
        jnp.zeros((head_count, DK, DK), jnp.float32),
    )
    (device_transition, device_update), unused = lax.scan(fold_span, identity_maps, (trans, write))

    def chain_step(hop_index, incoming_state):
        outgoing_state = (
            outer_product("eat,eto->eao", device_transition, incoming_state) + device_update
        )
        return from_behind(outgoing_state, "seq", 1)

    state_in = lax.fori_loop(0, lax.axis_size("seq") - 1, chain_step, jnp.zeros_like(device_update))

    def advance(memory_state, state_pair):
        return (
            outer_product("eat,eto->eao", state_pair[0], memory_state) + state_pair[1],
            memory_state,
        )

    unused_end, entry_states = lax.scan(advance, state_in, (trans, write))
    attended = out_local + outer_product("nhik,nhkv->nhiv", query_link, entry_states)
    corrected_values = u_local - outer_product("nhik,nhkv->nhiv", w_link, entry_states)
    positions = (first_position + jnp.arange(row_count, dtype=jnp.int32)).reshape(span_count, SPAN)
    last_tok = seg_ends - 1
    at_end = (positions[None] == last_tok[:, None, None]).astype(jnp.float32)
    ends_here = jnp.sum(at_end, axis=2)
    request_ids = jnp.arange(REQS, dtype=jnp.int32)
    member = (seg_blocks[None] == request_ids[:, None, None]).astype(jnp.float32) * ends_here[
        ..., None
    ]
    carried = jnp.sum(at_end * coupled_entries[None], axis=2)
    req_states = outer_product("rn,nhkv->rhkv", carried, entry_states)
    req_states = req_states + jnp.einsum(
        "rnj,nhjk,nhjv->rhkv", member, keys_b, corrected_values, precision=lax.Precision.HIGHEST
    )
    owned = (last_tok >= first_position) & (last_tok < first_position + row_count)
    wanted = last_tok[:, None] - rim_rows + 1 + jnp.arange(rim_rows, dtype=jnp.int32)[None, :]
    select = (
        (ext_pos[None, None, :] == wanted[:, :, None])
        & (ext_seg[None, None, :] == request_ids[:, None, None])
        & owned[:, None, None]
    )
    edge_vals = jnp.einsum(
        "rim,mcj->ricj", select.astype(jnp.bfloat16), extended, preferred_element_type=jnp.float32
    )
    totals = (
        lax.psum(req_states.astype(jnp.bfloat16), "seq").astype(jnp.float32),
        lax.psum(edge_vals.astype(jnp.bfloat16), "seq").astype(jnp.float32),
    )
    final_states = totals[0]
    conv_edges = totals[1].astype(jnp.bfloat16)
    heads_rows = attended.transpose(0, 2, 1, 3).reshape(row_count, head_count, DK)
    scale_heads = jnp.sqrt(jnp.mean(heads_rows * heads_rows, axis=-1, keepdims=True) + 1e-05)
    normed_heads = (
        (heads_rows / scale_heads * out_gain).reshape(row_count, local_width).astype(jnp.bfloat16)
    )
    mixed = lax.psum_scatter(
        jnp.dot(normed_heads, w_out, preferred_element_type=jnp.float32).astype(jnp.bfloat16),
        ("win", "wout"),
        scatter_dimension=0,
        tiled=True,
    ).astype(jnp.float32)
    summed = hidden_in.astype(jnp.float32) + mixed
    stream_out = summed.astype(jnp.bfloat16)
    scale_stream = jnp.sqrt(jnp.mean(summed * summed, axis=-1, keepdims=True) + 1e-05)
    normed_stream = (summed / scale_stream * norm_gain).astype(jnp.bfloat16)
    in_block = w_qkv.shape[0]
    all_rows = lax.all_gather(normed_stream, ("win", "wout"), axis=0, tiled=True)
    columns = lax.dynamic_slice_in_dim(all_rows, lax.axis_index("win") * in_block, in_block, 1)
    projected = lax.psum_scatter(
        jnp.dot(columns, w_qkv, preferred_element_type=jnp.float32).astype(jnp.bfloat16),
        "win",
        scatter_dimension=0,
        tiled=True,
    )
    return (projected, stream_out, final_states, conv_edges)


def solution(mesh):
    return jax.shard_map(
        body,
        mesh=mesh,
        in_specs=(
            P("seq", None, ("win", "wout")),
            P(None, None, ("win", "wout")),
            P(("win", "wout"), "seq"),
            P(),
            P(),
            P(("win", "wout"), None),
            P(("seq", "win", "wout"), None),
            P(),
            P("win", "wout"),
        ),
        out_specs=(
            P(("seq", "win"), "wout"),
            P(("seq", "win", "wout"), None),
            P(None, ("win", "wout"), None, None),
            P(None, None, None, ("win", "wout")),
        ),
        check_vma=False,
    )
```

profile of v0, /device:TPU:24, one launch (start us, length us, event | category | flops | bytes accessed | tf_op | source)
XLA Modules:
  0.0 252.5 jit_solution(6355066768874519596)
XLA Ops:
  8.1 0.9 slice.63
  8.9 1.4 collective-permute-start.1
  12.9 1.2 broadcast_bitcast_fusion
  15.2 0.9 fusion.87
  20.2 2.3 multiply_convert_fusion
  23.2 0.9 slice_convert_fusion
  24.1 1.8 mul.252
  25.9 2.0 reduce_sum.73
  27.9 1.6 add_sqrt_fusion.1
  29.5 1.6 copy.116
  31.9 1.3 reduce_sum.74
  33.9 1.1 reshape.343
  35.0 1.8 reshape.341
  36.8 1.8 reshape.342
  39.4 1.9 bitcast_multiply_fusion.2
  41.3 2.3 fusion.23
  43.5 40.7 %custom-call.3 = f32[4,2,1,64,64]{3,4,2,1,0:T(8,128)} custom-call(f32[4,2,1,64,64]{4,3,2,1,0:T(8,128)} %fusion.23), custom_call_target="InvertDiagBlocksLowerTriangular" | custom-call | tf_op jit(solution)/shard_map/triangular_solve | solution.py:85
  84.2 1.8 fusion.28
  86.0 1.8 convolution_multiply_fusion.1
  87.8 2.1 convolution_subtract_fusion.2
  89.9 1.1 fusion.56
  91.0 2.6 %fusion.48 = f32[4,2,128,128]{3,2,1,0:T(8,128)} fusion(f32[4,64,2,128]{3,1,2,0:T(8,128)S(1)} %get-tuple-element.164, f32[4,2,64,256]{3,2,1,0:T(8,128)S(1)} %fusion.28, f32[4,64]{1,0:T(4,128)} %get-tuple-element.176), kind=kOutput, calls=%fused_computation.72 | convolution fusion | flops 100728832 | bytes 1049600 | tf_op jit(solution)/shard_map/nhjk,nhjv->nhkv/dot_general | solution.py:28
  93.5 2.5 fusion.15
  96.0 9.9 %while.37 = (s32[]{:T(128)}, f32[2,128,128]{2,1,0:T(8,128)S(1)}, f32[2,128,128]{2,1,0:T(8,128)S(1)}, f32[4,2,128,128]{3,2,1,0:T(8,128)}, f32[4,2,128,128]{3,2,1,0:T(8,128)}, /*index=5*/s32[]{:T(128)}, s32[]{:T(128)}) while((s32[]{:T(128)}, f32[2,128,128]{2,1,0:T(8,128)S(1)}, f32[2,128,128]{2,1,0:T(8,128)S(1)}, ...), condition=%wide.region_6.7_spmd.clone, body=%wide.region_5.6_spmd.clone.sunk | while | flops 100728832 | bytes 1443426 | solution.py:116
  96.1 1.2 convolution_add_fusion.10
  97.3 1.2 fusion.117
  98.6 1.2 convolution_add_fusion.10
  99.8 1.2 fusion.117
  101.0 1.2 convolution_add_fusion.10
  102.3 1.2 fusion.117
  103.5 1.2 convolution_add_fusion.10
  104.8 1.2 fusion.117
  106.0 24.9 %while.35 = (s32[]{:T(128)}, f32[2,128,128]{2,1,0:T(8,128)S(1)}, f32[2,128,128]{2,1,0:T(8,128)S(1)}, f32[2,128,128]{2,1,0:T(8,128)S(1)}, s32[]{:T(128)}) while((s32[]{:T(128)}, f32[2,128,128]{2,1,0:T(8,128)S(1)}, f32[2,128,128]{2,1,0:T(8,128)S(1)}, f32[2,128,128]{2,1,0:T(8,128)S(1)}, s32[]{:T(128)}) %tuple.81), condition=%wide.region_8.9_spmd, body=%wide.region_7.8_spmd.sunk | while | flops 50364416 | bytes 1048677 | solution.py:124
  106.0 0.9 convolution_add_fusion.8
  106.9 1.3 collective-permute-start
  108.2 6.7 %collective-permute-done = f32[2,128,128]{2,1,0:T(8,128)S(1)} collective-permute-done((f32[2,128,128]{2,1,0:T(8,128)}, f32[2,128,128]{2,1,0:T(8,128)S(1)}, u32[]{:S(2)}, u32[]{:S(2)}) %collective-permute-start) | collective-permute-done | bytes 131104 | tf_op jit(solution)/shard_map/while/body/eval_jaxpr/ppermute | solution.py:15
  114.9 0.9 convolution_add_fusion.8
  115.8 1.3 collective-permute-start
  117.1 5.8 %collective-permute-done = f32[2,128,128]{2,1,0:T(8,128)S(1)} collective-permute-done((f32[2,128,128]{2,1,0:T(8,128)}, f32[2,128,128]{2,1,0:T(8,128)S(1)}, u32[]{:S(2)}, u32[]{:S(2)}) %collective-permute-start) | collective-permute-done | bytes 131104 | tf_op jit(solution)/shard_map/while/body/eval_jaxpr/ppermute | solution.py:15
  122.9 0.9 convolution_add_fusion.8
  123.8 1.3 collective-permute-start
  125.1 5.8 %collective-permute-done = f32[2,128,128]{2,1,0:T(8,128)S(1)} collective-permute-done((f32[2,128,128]{2,1,0:T(8,128)}, f32[2,128,128]{2,1,0:T(8,128)S(1)}, u32[]{:S(2)}, u32[]{:S(2)}) %collective-permute-start) | collective-permute-done | bytes 131104 | tf_op jit(solution)/shard_map/while/body/eval_jaxpr/ppermute | solution.py:15
  130.9 7.7 %while.36 = (s32[]{:T(128)}, f32[2,128,128]{2,1,0:T(8,128)S(1)}, f32[4,2,128,128]{3,2,1,0:T(8,128)}, f32[4,2,128,128]{3,2,1,0:T(8,128)}, f32[4,2,128,128]{3,2,1,0:T(8,128)}, /*index=5*/s32[]{:T(128)}) while((s32[]{:T(128)}, f32[2,128,128]{2,1,0:T(8,128)S(1)}, f32[4,2,128,128]{3,2,1,0:T(8,128)}, f32[4,2,128,128]{3,2,1,0:T(8,128)}, ...), condition=%wide.region_10.11_spmd, body=%wide.region_9.10_spmd.sunk | while | flops 50364416 | bytes 1049681 | solution.py:132
  131.5 1.2 convolution_add_fusion.9
  133.5 1.2 convolution_add_fusion.9
  135.4 1.2 convolution_add_fusion.9
  137.3 1.2 convolution_add_fusion.9
  138.6 2.4 multiply_reduce_fusion.1
  141.9 1.2 copy.124
  143.0 1.3 div.64
  144.3 2.7 %convolution_convert_fusion.1 = bf16[256,2048]{1,0:T(8,128)(2,1)} fusion(bf16[256,2048]{1,0:T(8,128)(2,1)} %param.20, f32[32,8,2,128]{3,2,1,0:T(2,128)S(1)} %bitcast.145, f32[32,8,2,128]{3,2,1,0:T(2,128)S(1)} %bitcast.144, f32[256]{0:T(256)} %broadcast_bitcast_fusion), kind=kOutput, calls=%fused_computation.20 | convolution fusion | flops 269156352 | bytes 2622464 | tf_op jit(solution)/shard_map/dot_general | solution.py:170
  147.0 37.4 %reduce-scatter.3.cloned.1.call-done = bf16[32,2048]{1,0:T(8,128)(2,1)} async-done(((bf16[256,2048]{1,0:T(8,128)(2,1)}), bf16[32,2048]{1,0:T(8,128)(2,1)}) %reduce-scatter.3.cloned.1.call-update) | async-done | bytes 131088 | tf_op jit(solution)/shard_map/reduce_scatter | solution.py:169
  184.5 1.1 multiply_reduce_fusion
  185.5 1.7 fusion.51
  187.5 1.1 broadcast_add_fusion
  188.9 1.8 fusion.17
  190.7 2.0 convolution_bitcast_fusion
  192.7 3.2 %fusion.16 = bf16[4,2,128,128]{3,0,2,1:T(4,128)(2,1)} fusion(f32[2,128,4,128]{3,1,2,0:T(8,128)S(1)} %convolution_bitcast_fusion, f32[4,2,128,128]{3,2,1,0:T(8,128)} %get-tuple-element.84, f32[4,4]{1,0:T(4,128)S(1)} %fusion.78), kind=kOutput, calls=%fused_computation.25 | convolution fusion | flops 6553600 | bytes 1310784 | tf_op jit(solution)/shard_map/rn,nhkv->rhkv/dot_general | solution.py:28
  196.0 14.8 %all-gather.2.cloned.1.call-done = bf16[256,2048]{1,0:T(8,128)(2,1)} async-done(((bf16[32,2048]{1,0:T(8,128)(2,1)}), bf16[256,2048]{1,0:T(8,128)(2,1)}) %all-gather.2.cloned.1.call-update) | async-done | bytes 1048592 | tf_op jit(solution)/shard_map/all_gather | solution.py:180
  210.9 3.1 %convolution_convert_fusion = bf16[256,3072]{1,0:T(8,128)(2,1)} fusion(bf16[512,3072]{1,0:T(8,128)(2,1)S(1)} %copy-done, bf16[256,2048]{1,0:T(8,128)(2,1)} %all-gather.2.cloned.1.call-done, s32[]{:T(128)S(6)} %select_n.21), kind=kOutput, calls=%fused_computation.19 | convolution fusion | flops 806092800 | bytes 4980740 | tf_op jit(solution)/shard_map/dot_general | solution.py:183
  215.3 0.9 convolution_convert_fusion.2
  216.1 16.8 %psum.15 = bf16[4,3,3,256]{3,0,2,1:T(4,128)(2,1)} all-reduce(bf16[4,3,3,256]{3,0,2,1:T(4,128)(2,1)} %convolution_convert_fusion.2), channel_id=1, replica_groups=mesh['seq'=4,'win'=4,'wout'=2] {'seq'}, use_global_device_ids=true, to_apply=%region_18.19 | all-reduce | flops 9216 | bytes 36864 | tf_op jit(solution)/shard_map/psum | solution.py:160
  232.9 1.8 copy.131
  234.7 10.7 %reduce-scatter.5.cloned.1.call-done = bf16[64,3072]{1,0:T(8,128)(2,1)} async-done(((bf16[256,3072]{1,0:T(8,128)(2,1)}), bf16[64,3072]{1,0:T(8,128)(2,1)}) %reduce-scatter.5.cloned.1.call-update) | async-done | bytes 393232 | tf_op jit(solution)/shard_map/reduce_scatter | solution.py:182
  (95 shorter events, 16.4 us)
Async XLA Ops:
  8.0 202.9 %copy-start = (bf16[512,3072]{1,0:T(8,128)(2,1)S(1)}, bf16[512,3072]{1,0:T(8,128)(2,1)}, u32[]{:S(2)}) copy-start(bf16[512,3072]{1,0:T(8,128)(2,1)} %param.23) | copy-start | bytes 9437188
  8.0 176.4 %reduce-scatter.3.cloned.1.call-start = ((), (), s32[]{:S(2)}) async-start(), calls=%async_computation.2 | async-start | bytes 1179648 | tf_op jit(solution)/shard_map/reduce_scatter | solution.py:169
  8.9 10.7 %collective-permute-start.1 = (bf16[3,3,256]{2,0,1:T(4,128)(2,1)S(1)}, bf16[3,3,256]{2,0,1:T(4,128)(2,1)S(1)}, u32[]{:S(2)}, u32[]{:S(2)}) collective-permute-start(bf16[3,3,256]{2,0,1:T(4,128)(2,1)S(1)} %slice.63), channel_id=1, source_target_pairs={{0,8},{8,16},{16,24},{1,9},{9,17},{17,25},{2,10},{10,18},{18,26},{... | collective-permute-start | bytes 13832 | tf_op jit(solution)/shard_map/ppermute | solution.py:15
  10.4 4.0 %copy-start.8 = (s32[259]{0:T(512)}, s32[259]{0:T(512)S(1)}, u32[]{:S(2)}) copy-start(s32[259]{0:T(512)S(1)} %iota_add_fusion.1) | copy-start | bytes 3112
  11.2 3.9 %copy-start.12 = (s32[4,1]{0,1:T(1,128)}, s32[4,1]{0,1:T(1,128)S(1)}, u32[]{:S(2)}) copy-start(s32[4,1]{0,1:T(1,128)S(1)} %reduce-window.7) | copy-start | bytes 52
  19.6 0.6 copy-start.10
  41.3 52.3 %copy-start.1 = (f32[4,64,2,128]{3,1,2,0:T(8,128)}, f32[4,64,2,128]{3,1,2,0:T(8,128)S(1)}, u32[]{:S(2)}) copy-start(f32[4,64,2,128]{3,1,2,0:T(8,128)S(1)} %get-tuple-element.164) | copy-start | bytes 786436
  84.2 9.3 %copy-start.5 = (f32[128,128]{1,0:T(8,128)S(1)}, f32[128,128]{1,0:T(8,128)}, u32[]{:S(2)}) copy-start(f32[128,128]{1,0:T(8,128)} %fusion.63) | copy-start | bytes 196612
  86.0 10.0 %copy-start.3 = (f32[4,2,64,256]{3,2,1,0:T(8,128)}, f32[4,2,64,256]{3,2,1,0:T(8,128)S(1)}, u32[]{:S(2)}) copy-start(f32[4,2,64,256]{3,2,1,0:T(8,128)S(1)} %fusion.28) | copy-start | bytes 1572868
  106.9 8.0 %collective-permute-start = (f32[2,128,128]{2,1,0:T(8,128)}, f32[2,128,128]{2,1,0:T(8,128)S(1)}, u32[]{:S(2)}, u32[]{:S(2)}) collective-permute-start(f32[2,128,128]{2,1,0:T(8,128)} %convolution_add_fusion.8), channel_id=1, source_target_pairs={{0,8},{8,16},{16,24},{1,9},{9,17},{17,25},{2,10},{10,18},{18,26},{... | collective-permute-start | bytes 393224 | tf_op jit(solution)/shard_map/while/body/eval_jaxpr/ppermute | solution.py:15
  115.8 7.1 %collective-permute-start = (f32[2,128,128]{2,1,0:T(8,128)}, f32[2,128,128]{2,1,0:T(8,128)S(1)}, u32[]{:S(2)}, u32[]{:S(2)}) collective-permute-start(f32[2,128,128]{2,1,0:T(8,128)} %convolution_add_fusion.8), channel_id=1, source_target_pairs={{0,8},{8,16},{16,24},{1,9},{9,17},{17,25},{2,10},{10,18},{18,26},{... | collective-permute-start | bytes 393224 | tf_op jit(solution)/shard_map/while/body/eval_jaxpr/ppermute | solution.py:15
  123.8 7.1 %collective-permute-start = (f32[2,128,128]{2,1,0:T(8,128)}, f32[2,128,128]{2,1,0:T(8,128)S(1)}, u32[]{:S(2)}, u32[]{:S(2)}) collective-permute-start(f32[2,128,128]{2,1,0:T(8,128)} %convolution_add_fusion.8), channel_id=1, source_target_pairs={{0,8},{8,16},{16,24},{1,9},{9,17},{17,25},{2,10},{10,18},{18,26},{... | collective-permute-start | bytes 393224 | tf_op jit(solution)/shard_map/while/body/eval_jaxpr/ppermute | solution.py:15
  130.9 7.7 %copy-start.4 = (f32[4,2,64,128]{3,2,1,0:T(8,128)S(1)}, f32[4,2,64,128]{3,2,1,0:T(8,128)}, u32[]{:S(2)}) copy-start(f32[4,2,64,128]{3,2,1,0:T(8,128)} %fusion.56) | copy-start | bytes 786436
  138.6 45.9 %copy-start.6 = (bf16[32,2048]{1,0:T(8,128)(2,1)S(1)}, bf16[32,2048]{1,0:T(8,128)(2,1)}, u32[]{:S(2)}) copy-start(bf16[32,2048]{1,0:T(8,128)(2,1)} %param.21) | copy-start | bytes 393220
  143.0 47.6 %copy-start.2 = (f32[4,64,2,128]{3,1,2,0:T(8,128)S(1)}, f32[4,64,2,128]{3,1,2,0:T(8,128)}, u32[]{:S(2)}) copy-start(f32[4,64,2,128]{3,1,2,0:T(8,128)} %copy-done.1) | copy-start | bytes 786436
  147.0 63.9 %all-gather.2.cloned.1.call-start = ((), (), s32[]{:S(2)}) async-start(), calls=%async_computation.3 | async-start | bytes 1179648 | tf_op jit(solution)/shard_map/all_gather | solution.py:180
  187.2 45.7 %all-reduce.2.cloned.1.call-start = ((), (), s32[]{:S(2)}) async-start(), calls=%async_computation.5 | async-start | bytes 524288 | tf_op jit(solution)/shard_map/psum | solution.py:159
  195.9 19.3 %copy-start.7 = (bf16[256,3,256]{2,0,1:T(8,128)(2,1)S(1)}, bf16[256,3,256]{2,0,1:T(8,128)(2,1)}, u32[]{:S(2)}) copy-start(bf16[256,3,256]{2,0,1:T(8,128)(2,1)} %param.15) | copy-start | bytes 1179652
  195.9 19.3 %copy-start.9 = (s32[259]{0:T(512)S(1)}, s32[259]{0:T(512)}, u32[]{:S(2)}) copy-start(s32[259]{0:T(512)} %copy-done.8) | copy-start | bytes 3112
  195.9 19.3 %copy-start.11 = (bf16[3,3,256]{2,0,1:T(4,128)(2,1)S(1)}, bf16[3,3,256]{2,0,1:T(4,128)(2,1)}, u32[]{:S(2)}) copy-start(bf16[3,3,256]{2,0,1:T(4,128)(2,1)} %copy-done.10) | copy-start | bytes 13828
  196.0 49.4 %reduce-scatter.5.cloned.1.call-start = ((), (), s32[]{:S(2)}) async-start(), calls=%async_computation.4 | async-start | bytes 1966080 | tf_op jit(solution)/shard_map/reduce_scatter | solution.py:182
Sparse Core Ops, SparseCore 0:
  147.1 37.3 reduce-scatter.2
  187.3 23.4 all-gather.1
  214.4 30.9 reduce-scatter.4
Sparse Core Ops, SparseCore 1:
  196.0 34.0 all-reduce.1
where the time goes:
time: 256 us; the launch traced here: 253 us
  waiting for transfers between devices  81.2 us (32%)
  other arithmetic  63.6 us (25%)
  matrix products  47.4 us (19%)
  local copies, waits for them, and re-layouts  22.1 us (9%)
  blocking collectives  16.8 us (7%)
  between operations  15.5 us (6%)
  starting transfers between devices  5.6 us (2%)
    another operation x4, other arithmetic, body(): lax.linalg.triangular_solve(system, targets, left_side=True, lower=True,...  42 us
    reduce_scatter x1, waiting for transfers between devices, body(): lax.psum_scatter(jnp.dot(normed_heads, w_out, preferred_element_type=jnp....  37.4 us
    dot_general x24, matrix products, outer_product(): return jnp.einsum(form, left, right, precision=lax.Precision.HIGHEST)  37.1 us
    ppermute x4, waiting for transfers between devices, from_behind(): lax.ppermute(value, axis, [(source, source + steps) for source in range(l...  18.2 us
    psum x1, blocking collectives, body(): lax.psum(edge_vals.astype(jnp.bfloat16), 'seq').astype(jnp.float32)  16.8 us
    all_gather x1, waiting for transfers between devices, body(): lax.all_gather(normed_stream, ('win', 'wout'), axis=0, tiled=True)  14.8 us
    reduce_scatter x1, waiting for transfers between devices, body(): lax.psum_scatter(jnp.dot(columns, w_qkv, preferred_element_type=jnp.float...  10.7 us
    ppermute x4, starting transfers between devices, from_behind(): lax.ppermute(value, axis, [(source, source + steps) for source in range(l...  5.25 us
  transfers between devices with their start and end apart: 8, of which 6 were waited for; matrix products, arithmetic and copies ran while one was open for 10% of the time, Pallas kernels for 0%

commit v1 on v0

v1 whole, which is shorter than its diff:
```python
import functools

import jax
import jax.numpy as jnp
from jax import lax
from jax.experimental import pallas as pl
from jax.experimental.pallas import tpu as pltpu
from jax.sharding import PartitionSpec as P

MESH = pl.DeviceIdType.MESH
DK = 128
CONV = 4
HALO = 16
F32 = jnp.float32
BF16 = jnp.bfloat16


def dot(a, b):
    return jnp.dot(a, b, preferred_element_type=F32)


def dot_t(a, b):
    return lax.dot_general(a, b, (((1,), (1,)), ((), ())), preferred_element_type=F32)


def split(x):
    high = x.astype(BF16)
    return high, (x - high.astype(F32)).astype(BF16)


def mm3(a, b, product=dot):
    ah, al = split(a)
    bh, bl = split(b)
    return product(ah, bh) + (product(ah, bl) + product(al, bh))


def kernel(
    n, wins, reqs,
    lengths, qkv, conv_w, beta, out_gain, hidden, norm_gain, w_out, w_qkv,
    qkv_next, stream_out, fs_out, edge_out,
    halo, wo_own, wo_sib, wq, state_send, state_recv, nh, nh_send, nh_recv,
    part_keep, part_send, part_recv, ns, gathered, proj_send, proj_recv,
    res, up_send, up_recv, down_send, down_recv,
    local_sem, halo_sem, wo_sem, state_sem, nh_sem, part_send_sem, part_recv_sem,
    ns_send_sem, ns_recv_sem, proj_send_sem, proj_recv_sem, up_sem, down_sem,
):
    rows = qkv.shape[1]
    width = qkv.shape[2]
    heads = width // DK
    half = rows // 2
    group = wins * 2
    blk = hidden.shape[0]
    k_idx = lax.axis_index("seq")
    w = lax.axis_index("win")
    c = lax.axis_index("wout")
    me = w * 2 + c
    sib = {"wout": 1 - c}
    above = {"seq": lax.rem(k_idx + 1, n)}
    below = {"seq": lax.rem(k_idx + n - 1, n)}
    not_first = k_idx > 0
    not_last = k_idx < n - 1

    def remote(src, dst, send_sem, recv_sem, device):
        return pltpu.make_async_remote_copy(
            src_ref=src, dst_ref=dst, send_sem=send_sem, recv_sem=recv_sem,
            device_id=device, device_id_type=MESH,
        )

    def peer(o):
        p = lax.rem(me + o, group)
        return p // 2, lax.rem(p, 2)

    barrier = pltpu.get_barrier_semaphore()
    for o in range(1, group):
        pw, pc = peer(o)
        pl.semaphore_signal(barrier, inc=1, device_id={"win": pw, "wout": pc}, device_id_type=MESH)

    @pl.when(not_first)
    def _():
        pl.semaphore_signal(barrier, inc=1, device_id=below, device_id_type=MESH)

    @pl.when(not_last)
    def _():
        pl.semaphore_signal(barrier, inc=1, device_id=above, device_id_type=MESH)

    copy_wo = pltpu.make_async_copy(w_out, wo_own, local_sem.at[0])
    copy_wq = pltpu.make_async_copy(w_qkv, wq, local_sem.at[1])
    copy_wo.start()
    copy_wq.start()
    pl.semaphore_wait(
        barrier, group - 1 + not_first.astype(jnp.int32) + not_last.astype(jnp.int32)
    )

    halo_copy = remote(
        qkv.at[:, pl.ds(rows - HALO, HALO), :], halo, halo_sem.at[0], halo_sem.at[1], above
    )

    @pl.when(not_last)
    def _():
        halo_copy.start()

    wo_copy = remote(w_out, wo_sib, wo_sem.at[0], wo_sem.at[1], sib)
    wo_copy.start()

    @pl.when(jnp.logical_not(not_first))
    def _():
        halo[...] = jnp.zeros_like(halo)
        state_recv[...] = jnp.zeros_like(state_recv)

    ends = []
    total = jnp.int32(0)
    for r in range(reqs):
        total = total + lengths[r]
        ends.append(total)
    first = k_idx * rows

    def segments(positions):
        seg = jnp.zeros_like(positions)
        for r in range(reqs):
            seg = seg + (positions >= ends[r]).astype(jnp.int32)
        return jnp.where(positions < 0, -1, seg)

    def scalar_segment(position):
        seg = jnp.int32(0)
        for r in range(reqs):
            seg = seg + (position >= ends[r]).astype(jnp.int32)
        return jnp.where(position < 0, -1, seg)

    col_pos = first + lax.broadcasted_iota(jnp.int32, (rows, 1), 0)
    row_pos = first + lax.broadcasted_iota(jnp.int32, (1, rows), 1)
    col_seg = segments(col_pos)
    row_seg = segments(row_pos)
    before_seg = scalar_segment(first - 1)
    last_seg = scalar_segment(first + rows - 1)
    coupled = (col_seg == before_seg).astype(F32)
    in_last = (row_seg == last_seg).astype(F32)
    last_link = (before_seg == last_seg).astype(F32)

    ri = lax.broadcasted_iota(jnp.int32, (rows, rows), 0)
    ci = lax.broadcasted_iota(jnp.int32, (rows, rows), 1)
    same = col_seg == row_seg
    causal = same & (ri >= ci)
    strict = same & (ri > ci)
    diagonal = ri == ci
    hi_ = lax.broadcasted_iota(jnp.int32, (half, half), 0)
    hj_ = lax.broadcasted_iota(jnp.int32, (half, half), 1)
    eye_half = (hi_ == hj_).astype(F32)
    eye_keys = (
        lax.broadcasted_iota(jnp.int32, (DK, DK), 0) == lax.broadcasted_iota(jnp.int32, (DK, DK), 1)
    ).astype(F32)

    @pl.when(not_first)
    def _():
        halo_copy.wait_recv()

    activated = []
    extended = []
    for t in range(3):
        ext = jnp.concatenate([halo[t], qkv[t]], axis=0)
        extended.append(ext)
        wide = ext.astype(F32)
        pre = conv_w[t, CONV - 1 : CONV, :] * wide[HALO:]
        for back in range(1, CONV):
            shifted = pltpu.roll(wide, back, axis=0)[HALO:]
            keep = segments(col_pos - back) == col_seg
            pre = pre + conv_w[t, CONV - 1 - back : CONV - back, :] * jnp.where(keep, shifted, 0.0)
        activated.append((pre / (1.0 + jnp.exp(-pre))).astype(BF16).astype(F32))

    def unit(x):
        return x * lax.rsqrt(jnp.sum(x * x, axis=-1, keepdims=True) + 1e-6)

    q, k, v, kt, a_full, scores, strength = [], [], [], [], [], [], []
    for h in range(heads):
        cols = slice(h * DK, (h + 1) * DK)
        q.append(unit(activated[0][:, cols]))
        k.append(unit(activated[1][:, cols]))
        v.append(activated[2][:, cols])
        b_row = 1.0 / (1.0 + jnp.exp(-beta[h : h + 1, :]))
        b_col = jnp.sum(jnp.where(diagonal, b_row, 0.0), axis=1, keepdims=True)
        strength.append(b_col)
        kt.append(jnp.transpose(k[h]))
        gram = mm3(k[h], k[h], dot_t)
        a_full.append(jnp.where(strict, b_col * gram, 0.0))
        scores.append(jnp.where(causal, mm3(q[h], k[h], dot_t), 0.0))

    diag = []
    for h in range(heads):
        diag.append(a_full[h][:half, :half])
        diag.append(a_full[h][half:, half:])
    level = 0
    inverse = None
    while (1 << level) < half:
        pick = (
            ((hi_ >> (level + 1)) == (hj_ >> (level + 1)))
            & (((hi_ >> level) & 1) == 1)
            & (((hj_ >> level) & 1) == 0)
        )
        lower = [jnp.where(pick, a, 0.0) for a in diag]
        if level == 0:
            inverse = [eye_half - x for x in lower]
        else:
            ys = [mm3(x, z) for x, z in zip(lower, inverse)]
            inverse = [z - mm3(z, y) for z, y in zip(inverse, ys)]
        level += 1

    solved, out_local, q_link, trans, write = [], [], [], [], []
    for h in range(heads):
        rhs = jnp.concatenate([strength[h] * v[h], (strength[h] * coupled) * k[h]], axis=1)
        top = mm3(inverse[2 * h], rhs[:half])
        low = mm3(inverse[2 * h + 1], rhs[half:] - mm3(a_full[h][half:, :half], top))
        solved.append(jnp.concatenate([top, low], axis=0))
    for h in range(heads):
        m = mm3(kt[h] * in_last, solved[h])
        write.append(m[:, :DK])
        trans.append(last_link * (eye_keys - m[:, DK:]))

    state_copy = remote(state_send, state_recv, state_sem.at[0], state_sem.at[1], above)

    @pl.when(not_first)
    def _():
        state_copy.wait_recv()

    state_in = [state_recv[h * DK : (h + 1) * DK, :].astype(F32) for h in range(heads)]
    for h in range(heads):
        state_send[h * DK : (h + 1) * DK, :] = (mm3(trans[h], state_in[h]) + write[h]).astype(BF16)

    @pl.when(not_last)
    def _():
        state_copy.start()

    corrected = []
    for h in range(heads):
        s = mm3(scores[h], solved[h])
        link = jnp.concatenate([coupled * q[h] - s[:, DK:], solved[h][:, DK:]], axis=0)
        applied = mm3(link, state_in[h])
        att = s[:, :DK] + applied[:rows]
        corrected.append(solved[h][:, :DK] - applied[rows:])
        scale = lax.rsqrt(jnp.mean(att * att, axis=-1, keepdims=True) + 1e-5)
        nh[:, h * DK : (h + 1) * DK] = (att * scale * out_gain[...]).astype(BF16)

    for o in range(wins):
        start = pl.multiple_of((2 * o + 1 - c) * blk, blk)
        nh_send[o * blk : (o + 1) * blk, :] = nh[pl.ds(start, blk), :]
    nh_copy = remote(nh_send, nh_recv, nh_sem.at[0], nh_sem.at[1], sib)
    nh_copy.start()
    own_rows = jnp.concatenate(
        [nh[pl.ds(pl.multiple_of((2 * o + c) * blk, blk), blk), :] for o in range(wins)], axis=0
    )
    copy_wo.wait()
    wo_copy.wait_recv()
    part_keep[...] = dot(own_rows, wo_own[...])
    nh_copy.wait_recv()
    part_keep[...] = part_keep[...] + dot(nh_recv[...], wo_sib[...])
    part_copies = []
    for o in range(1, wins):
        pw = lax.rem(w + o, wins)
        part_send[o] = part_keep[pl.ds(pl.multiple_of(pw * blk, blk), blk), :].astype(BF16)
        cp = remote(
            part_send.at[o], part_recv.at[o], part_send_sem.at[o], part_recv_sem.at[o], {"win": pw}
        )
        cp.start()
        part_copies.append(cp)

    for r in range(reqs):
        owned = (ends[r] - 1 >= first) & (ends[r] - 1 < first + rows)
        owned_f = owned.astype(F32)
        member = (row_seg == r).astype(F32) * owned_f
        carry = owned_f * (before_seg == r).astype(F32)
        for h in range(heads):
            base = (r * heads + h) * DK
            res[base : base + DK, :] = (
                mm3(kt[h] * member, corrected[h]) + carry * state_in[h]
            ).astype(BF16)
    edge_base = reqs * heads * DK
    sel_row = lax.broadcasted_iota(jnp.int32, (16, HALO + rows), 0)
    sel_pos = first - HALO + lax.broadcasted_iota(jnp.int32, (16, HALO + rows), 1)
    sel_seg = segments(sel_pos)
    select = jnp.zeros((16, HALO + rows), F32)
    for r in range(reqs):
        owned = (ends[r] - 1 >= first) & (ends[r] - 1 < first + rows)
        for i in range(CONV - 1):
            hit = (
                (sel_row == r * (CONV - 1) + i)
                & (sel_pos == ends[r] - (CONV - 1) + i)
                & (sel_seg == r)
            )
            select = select + jnp.where(hit, 1.0, 0.0) * owned.astype(F32)
    select = select.astype(BF16)
    pieces = width // DK
    for t in range(3):
        edge = dot(select, extended[t])
        for j in range(pieces):
            base = edge_base + (t * pieces + j) * 16
            res[base : base + 16, :] = edge[:, j * DK : (j + 1) * DK].astype(BF16)

    up_copy = remote(up_send, up_recv, up_sem.at[0], up_sem.at[1], above)
    down_copy = remote(down_send, down_recv, down_sem.at[0], down_sem.at[1], below)

    def up_step():
        up_copy.wait_recv()

        @pl.when(not_last)
        def _():
            up_send[...] = up_recv[...] + res[...]
            up_copy.start()

    def down_step():
        down_copy.wait_recv()

        @pl.when(not_first)
        def _():
            down_send[...] = down_recv[...] + res[...]
            down_copy.start()

    @pl.when(k_idx == 0)
    def _():
        up_recv[...] = jnp.zeros_like(up_recv)
        up_send[...] = res[...]
        up_copy.start()

    @pl.when(k_idx == n - 1)
    def _():
        down_recv[...] = jnp.zeros_like(down_recv)
        down_send[...] = res[...]
        down_copy.start()

    summed = hidden[...].astype(F32) + part_keep[pl.ds(pl.multiple_of(w * blk, blk), blk), :]
    for o in range(1, wins):
        part_copies[o - 1].wait_recv()
        summed = summed + part_recv[o].astype(F32)
    stream_out[...] = summed.astype(BF16)
    scale = lax.rsqrt(jnp.mean(summed * summed, axis=-1, keepdims=True) + 1e-5)
    ns[...] = (summed * scale * norm_gain[...]).astype(BF16)
    in_block = wq.shape[0]
    my_rows = pl.ds(pl.multiple_of(me * blk, blk), blk)
    ns_copies = []
    for o in range(1, group):
        pw, pc = peer(o)
        cp = remote(
            ns.at[:, pl.ds(pl.multiple_of(pw * in_block, in_block), in_block)],
            gathered.at[my_rows, :],
            ns_send_sem.at[o], ns_recv_sem.at[o], {"win": pw, "wout": pc},
        )
        cp.start()
        ns_copies.append(cp)
    gathered[my_rows, :] = ns[:, pl.ds(pl.multiple_of(w * in_block, in_block), in_block)]

    pl.when(k_idx == 1)(up_step)
    pl.when(k_idx == n - 2)(down_step)

    copy_wq.wait()
    for cp in ns_copies:
        cp.wait_recv()
    out_rows = blk * 2
    proj_copies = []
    for o in range(1, wins):
        pw = lax.rem(w + o, wins)
        block = gathered[pl.ds(pl.multiple_of(pw * out_rows, out_rows), out_rows), :]
        proj_send[o] = dot(block, wq[...]).astype(BF16)
        cp = remote(
            proj_send.at[o], proj_recv.at[o], proj_send_sem.at[o], proj_recv_sem.at[o], {"win": pw}
        )
        cp.start()
        proj_copies.append(cp)
    own = dot(gathered[pl.ds(pl.multiple_of(w * out_rows, out_rows), out_rows), :], wq[...])

    pl.when((k_idx == 2) & (k_idx > 1))(up_step)
    pl.when((k_idx == n - 3) & (k_idx < n - 2))(down_step)
    pl.when(k_idx > 2)(up_step)
    pl.when(k_idx < n - 3)(down_step)

    total_res = res[...].astype(F32) + up_recv[...].astype(F32) + down_recv[...].astype(F32)
    fs_out[...] = total_res[:edge_base]
    for t in range(3 * pieces):
        base = edge_base + t * 16
        edge_out[:, t * DK : (t + 1) * DK] = total_res[base : base + 16].astype(BF16)

    for cp in proj_copies:
        cp.wait_recv()
    for o in range(1, wins):
        own = own + proj_recv[o].astype(F32)
    qkv_next[...] = own.astype(BF16)

    wo_copy.wait_send()
    nh_copy.wait_send()
    for cp in part_copies + ns_copies + proj_copies:
        cp.wait_send()

    @pl.when(not_last)
    def _():
        halo_copy.wait_send()
        state_copy.wait_send()
        up_copy.wait_send()

    @pl.when(not_first)
    def _():
        down_copy.wait_send()


def solution(mesh):
    n, wins = mesh.shape["seq"], mesh.shape["win"]

    def body(qkv_in, conv_w, beta_logits, lengths, out_gain, w_out, hidden_in, norm_gain, w_qkv):
        rows, _, width = qkv_in.shape
        heads = width // DK
        reqs = lengths.shape[0]
        blk, model = hidden_in.shape
        in_block, out_cols = w_qkv.shape
        group = wins * 2
        res_rows = reqs * heads * DK + 16 * 3 * (width // DK)
        vmem = pl.BlockSpec(memory_space=pltpu.VMEM)
        dma = pltpu.SemaphoreType.DMA
        results = pl.pallas_call(
            functools.partial(kernel, n, wins, reqs),
            out_shape=(
                jax.ShapeDtypeStruct((blk * 2, out_cols), BF16),
                jax.ShapeDtypeStruct((blk, model), BF16),
                jax.ShapeDtypeStruct((reqs * heads * DK, DK), F32),
                jax.ShapeDtypeStruct((16, 3 * width), BF16),
            ),
            in_specs=[pl.BlockSpec(memory_space=pltpu.SMEM)] + [vmem] * 6
            + [pl.BlockSpec(memory_space=pl.ANY)] * 2,
            out_specs=(vmem,) * 4,
            scratch_shapes=[
                pltpu.VMEM((3, HALO, width), BF16),
                pltpu.VMEM((width, model), BF16),
                pltpu.VMEM((width, model), BF16),
                pltpu.VMEM((in_block, out_cols), BF16),
                pltpu.VMEM((heads * DK, DK), BF16),
                pltpu.VMEM((heads * DK, DK), BF16),
                pltpu.VMEM((rows, width), BF16),
                pltpu.VMEM((rows // 2, width), BF16),
                pltpu.VMEM((rows // 2, width), BF16),
                pltpu.VMEM((rows // 2, model), F32),
                pltpu.VMEM((wins, blk, model), BF16),
                pltpu.VMEM((wins, blk, model), BF16),
                pltpu.VMEM((blk, model), BF16),
                pltpu.VMEM((rows, in_block), BF16),
                pltpu.VMEM((wins, blk * 2, out_cols), BF16),
                pltpu.VMEM((wins, blk * 2, out_cols), BF16),
                pltpu.VMEM((res_rows, DK), BF16),
                pltpu.VMEM((res_rows, DK), BF16),
                pltpu.VMEM((res_rows, DK), BF16),
                pltpu.VMEM((res_rows, DK), BF16),
                pltpu.VMEM((res_rows, DK), BF16),
                dma((2,)), dma((2,)), dma((2,)), dma((2,)), dma((2,)),
                dma((wins,)), dma((wins,)), dma((group,)), dma((group,)),
                dma((wins,)), dma((wins,)), dma((2,)), dma((2,)),
            ],
            compiler_params=pltpu.CompilerParams(
                collective_id=0, has_side_effects=True, vmem_limit_bytes=56 * 1024 * 1024
            ),
            cost_estimate=pl.CostEstimate(
                flops=4 * 10**9, bytes_accessed=8 * 10**6, transcendentals=10**6
            ),
            name="delta_sublayer",
        )(
            lengths, jnp.transpose(qkv_in, (1, 0, 2)), conv_w, beta_logits,
            out_gain.reshape(1, DK), hidden_in, norm_gain.reshape(1, model), w_out, w_qkv,
        )
        projected, stream, states, edges = results
        taps = CONV - 1
        return (
            projected,
            stream,
            states.reshape(reqs, heads, DK, DK),
            edges[: reqs * taps].reshape(reqs, taps, 3, width),
        )

    return jax.shard_map(
        body,
        mesh=mesh,
        in_specs=(
            P("seq", None, ("win", "wout")),
            P(None, None, ("win", "wout")),
            P(("win", "wout"), "seq"),
            P(),
            P(),
            P(("win", "wout"), None),
            P(("seq", "win", "wout"), None),
            P(),
            P("win", "wout"),
        ),
        out_specs=(
            P(("seq", "win"), "wout"),
            P(("seq", "win", "wout"), None),
            P(None, ("win", "wout"), None, None),
            P(None, None, None, ("win", "wout")),
        ),
        check_vma=False,
    )
```

time: 256 us -> 62.7 us (0.24); the launches traced: 253 us -> 62.3 us
  waiting for transfers between devices: 81.2 us -> 0 us
  other arithmetic: 63.6 us -> 0 us
  Pallas kernels: 0 us -> 55.1 us
  matrix products: 47.4 us -> 0 us
  blocking collectives: 16.8 us -> 0 us
  local copies, waits for them, and re-layouts: 22.1 us -> 6.57 us
  between operations: 15.5 us -> 0.65 us
  starting transfers between devices: 5.6 us -> 0 us
    pallas_call x0 -> x1, Pallas kernels: none -> 55.1 us  [body(): pl.pallas_call(functools.partial(kernel, n, wins, reqs), out_shape=(jax.S...]
    reduce_scatter x2 -> x0, waiting for transfers between devices: 48.1 us -> none  [the longest x1 37.4 us: body(): lax.psum_scatter(jnp.dot(normed_heads, w_out, preferred_element_type=jnp....]
    dot_general x28 -> x0, matrix products: 45.7 us -> none  [the longest x24 37.1 us: outer_product(): return jnp.einsum(form, left, right, precision=lax.Precision.HIGHEST)]
    another operation x5 -> x0, other arithmetic: 42.8 us -> none  [the longest x4 42 us: body(): lax.linalg.triangular_solve(system, targets, left_side=True, lower=True,...]
    ppermute x4 -> x0, waiting for transfers between devices: 18.2 us -> none  [from_behind(): lax.ppermute(value, axis, [(source, source + steps) for source in range(l...]
    psum x1 -> x0, blocking collectives: 16.8 us -> none  [body(): lax.psum(edge_vals.astype(jnp.bfloat16), 'seq').astype(jnp.float32)]
    all_gather x1 -> x0, waiting for transfers between devices: 14.8 us -> none  [body(): lax.all_gather(normed_stream, ('win', 'wout'), axis=0, tiled=True)]
    convert_element_type x6 -> x0, other arithmetic: 6.16 us -> none  [the longest x1 2.33 us: body(): activated = jax.nn.silu(pre).astype(jnp.bfloat16)]
  transfers between devices with their start and end apart: 8 -> 0, of which waited for: 6 -> 0; matrix products, arithmetic and copies ran while one was open for 10% -> 0% of each run, Pallas kernels for 0% -> 0%
where the time goes in v1:
time: 62.7 us; the launch traced here: 62.3 us
  Pallas kernels  55.1 us (88%)
  local copies, waits for them, and re-layouts  6.57 us (10%)
  between operations  0.65 us (1%)
    pallas_call x1, Pallas kernels, body(): pl.pallas_call(functools.partial(kernel, n, wins, reqs), out_shape=(jax.S...  55.1 us
    unnamed x4, local copies, waits for them, and re-layouts  5.82 us

profile of v1, /device:TPU:24, one launch (start us, length us, event | category | flops | bytes accessed | tf_op | source)
XLA Modules:
  0.0 62.3 jit_solution(4384452873502319518)
XLA Ops:
  0.6 55.1 %delta_sublayer.1 = (bf16[64,3072]{1,0:T(8,128)(2,1)}, bf16[32,2048]{1,0:T(8,128)(2,1)}, f32[1024,128]{1,0:T(8,128)}, bf16[16,768]{1,0:T(8,128)(2,1)}) custom-call(s32[4]{0:T(128)} %lengths.1, bf16[3,256,256]{2,1,0:T(8,128)(2,1)} %bitcast.7, f32[3,4,256]{2,1,0:T(4,128)} %conv_w.1, f32[2,256]{1,0:T(2,128)} %beta.1, f32[1,128]{1,0:T(1,128)} %bitcast.9, ...), custom_call_target="tpu_custom_call" | custom-call | flops 4000000000 | bytes 8000000 | tf_op jit(solution)/shard_map/delta_sublayer/pallas_call | solution.py:413
  55.7 0.8 %reshape.23 = bf16[4,3,3,256]{3,2,1,0:T(4,128)(2,1)S(1)} reshape(bf16[12,768]{1,0:T(8,128)(2,1)} %bitcast.6) | data formatting | bytes 36864 | tf_op jit(solution)/shard_map/reshape | solution.py:467
  56.5 0.6 copy.14
  57.1 1.8 %copy.18 = bf16[64,3072]{1,0:T(8,128)(2,1)} copy(bf16[64,3072]{1,0:T(8,128)(2,1)} %get-tuple-element.24) | data formatting | bytes 786432
  58.9 1.6 %copy.19 = bf16[32,2048]{1,0:T(8,128)(2,1)} copy(bf16[32,2048]{1,0:T(8,128)(2,1)} %get-tuple-element.25) | data formatting | bytes 262144
  60.4 1.9 %copy.20 = f32[4,2,128,128]{3,2,1,0:T(8,128)} copy(f32[4,2,128,128]{3,2,1,0:T(8,128)} %bitcast.5) | data formatting | bytes 1048576

commit v2 on v1

--- a/solution.py
+++ b/solution.py
@@ -149,38 +149,58 @@
         lax.broadcasted_iota(jnp.int32, (DK, DK), 0) == lax.broadcasted_iota(jnp.int32, (DK, DK), 1)
     ).astype(F32)
 
+    def silu(x):
+        return (x / (1.0 + jnp.exp(-x))).astype(BF16).astype(F32)
+
+    index_col = lax.broadcasted_iota(jnp.int32, (rows, 1), 0)
+    keeps = [None] + [segments(col_pos - back) == col_seg for back in range(1, CONV)]
+
+    def tap(t, back):
+        return conv_w[t, CONV - 1 - back : CONV - back, :]
+
+    pres = []
+    mains = []
+    for t in range(3):
+        wide = qkv[t].astype(F32)
+        pre = tap(t, 0) * wide
+        for back in range(1, CONV):
+            shifted = pltpu.roll(wide, back, axis=0)
+            pre = pre + tap(t, back) * jnp.where(keeps[back] & (index_col >= back), shifted, 0.0)
+        pres.append(pre[:8])
+        mains.append(silu(pre)[8:])
+
+    strength = []
+    for h in range(heads):
+        b_row = 1.0 / (1.0 + jnp.exp(-beta[h : h + 1, :]))
+        strength.append(jnp.sum(jnp.where(diagonal, b_row, 0.0), axis=1, keepdims=True))
+
     @pl.when(not_first)
     def _():
         halo_copy.wait_recv()
 
     activated = []
-    extended = []
     for t in range(3):
-        ext = jnp.concatenate([halo[t], qkv[t]], axis=0)
-        extended.append(ext)
-        wide = ext.astype(F32)
-        pre = conv_w[t, CONV - 1 : CONV, :] * wide[HALO:]
+        rim = halo[t].astype(F32)[HALO - 8 :]
+        pre = pres[t]
         for back in range(1, CONV):
-            shifted = pltpu.roll(wide, back, axis=0)[HALO:]
-            keep = segments(col_pos - back) == col_seg
-            pre = pre + conv_w[t, CONV - 1 - back : CONV - back, :] * jnp.where(keep, shifted, 0.0)
-        activated.append((pre / (1.0 + jnp.exp(-pre))).astype(BF16).astype(F32))
+            shifted = pltpu.roll(rim, back, axis=0)
+            pre = pre + tap(t, back) * jnp.where(
+                keeps[back][:8] & (index_col[:8] < back), shifted, 0.0
+            )
+        activated.append(jnp.concatenate([silu(pre), mains[t]], axis=0))
 
     def unit(x):
         return x * lax.rsqrt(jnp.sum(x * x, axis=-1, keepdims=True) + 1e-6)
 
-    q, k, v, kt, a_full, scores, strength = [], [], [], [], [], [], []
+    q, k, v, kt, a_full, scores = [], [], [], [], [], []
     for h in range(heads):
         cols = slice(h * DK, (h + 1) * DK)
         q.append(unit(activated[0][:, cols]))
         k.append(unit(activated[1][:, cols]))
         v.append(activated[2][:, cols])
-        b_row = 1.0 / (1.0 + jnp.exp(-beta[h : h + 1, :]))
-        b_col = jnp.sum(jnp.where(diagonal, b_row, 0.0), axis=1, keepdims=True)
-        strength.append(b_col)
         kt.append(jnp.transpose(k[h]))
         gram = mm3(k[h], k[h], dot_t)
-        a_full.append(jnp.where(strict, b_col * gram, 0.0))
+        a_full.append(jnp.where(strict, strength[h] * gram, 0.0))
         scores.append(jnp.where(causal, mm3(q[h], k[h], dot_t), 0.0))
 
     diag = []
@@ -214,25 +234,36 @@
         write.append(m[:, :DK])
         trans.append(last_link * (eye_keys - m[:, DK:]))
 
-    state_copy = remote(state_send, state_recv, state_sem.at[0], state_sem.at[1], above)
-
-    @pl.when(not_first)
-    def _():
-        state_copy.wait_recv()
-
-    state_in = [state_recv[h * DK : (h + 1) * DK, :].astype(F32) for h in range(heads)]
-    for h in range(heads):
-        state_send[h * DK : (h + 1) * DK, :] = (mm3(trans[h], state_in[h]) + write[h]).astype(BF16)
-
-    @pl.when(not_last)
-    def _():
-        state_copy.start()
+    steps = n // 2
+    state_copies = [
+        remote(state_send.at[i], state_recv.at[i], state_sem.at[0, i], state_sem.at[1, i], above)
+        for i in range(steps)
+    ]
+    for i in range(steps):
+        if i > 0:
+            pl.when(not_first)(state_copies[i - 1].wait_recv)
+        for h in range(heads):
+            hr = slice(h * DK, (h + 1) * DK)
+            state = write[h]
+            if i > 0:
+                state = state + mm3(trans[h], state_recv[i - 1, hr, :].astype(F32))
+            state_send[i, hr, :] = state.astype(BF16)
+        pl.when(not_last)(state_copies[i].start)
+        if i == 0:
+            local = [mm3(scores[h], solved[h]) for h in range(heads)]
+            links = [
+                jnp.concatenate([coupled * q[h] - local[h][:, DK:], solved[h][:, DK:]], axis=0)
+                for h in range(heads)
+            ]
+    pl.when(not_first)(state_copies[steps - 1].wait_recv)
+    state_in = [
+        state_recv[steps - 1, h * DK : (h + 1) * DK, :].astype(F32) for h in range(heads)
+    ]
 
     corrected = []
     for h in range(heads):
-        s = mm3(scores[h], solved[h])
-        link = jnp.concatenate([coupled * q[h] - s[:, DK:], solved[h][:, DK:]], axis=0)
-        applied = mm3(link, state_in[h])
+        s = local[h]
+        applied = mm3(links[h], state_in[h])
         att = s[:, :DK] + applied[:rows]
         corrected.append(solved[h][:, :DK] - applied[rows:])
         scale = lax.rsqrt(jnp.mean(att * att, axis=-1, keepdims=True) + 1e-5)
@@ -272,23 +303,28 @@
                 mm3(kt[h] * member, corrected[h]) + carry * state_in[h]
             ).astype(BF16)
     edge_base = reqs * heads * DK
-    sel_row = lax.broadcasted_iota(jnp.int32, (16, HALO + rows), 0)
-    sel_pos = first - HALO + lax.broadcasted_iota(jnp.int32, (16, HALO + rows), 1)
-    sel_seg = segments(sel_pos)
-    select = jnp.zeros((16, HALO + rows), F32)
-    for r in range(reqs):
-        owned = (ends[r] - 1 >= first) & (ends[r] - 1 < first + rows)
-        for i in range(CONV - 1):
-            hit = (
-                (sel_row == r * (CONV - 1) + i)
-                & (sel_pos == ends[r] - (CONV - 1) + i)
-                & (sel_seg == r)
-            )
-            select = select + jnp.where(hit, 1.0, 0.0) * owned.astype(F32)
-    select = select.astype(BF16)
+
+    def selection(base, count):
+        sel_row = lax.broadcasted_iota(jnp.int32, (16, count), 0)
+        sel_pos = base + lax.broadcasted_iota(jnp.int32, (16, count), 1)
+        sel_seg = segments(sel_pos)
+        select = jnp.zeros((16, count), F32)
+        for r in range(reqs):
+            owned = (ends[r] - 1 >= first) & (ends[r] - 1 < first + rows)
+            for i in range(CONV - 1):
+                hit = (
+                    (sel_row == r * (CONV - 1) + i)
+                    & (sel_pos == ends[r] - (CONV - 1) + i)
+                    & (sel_seg == r)
+                )
+                select = select + jnp.where(hit, 1.0, 0.0) * owned.astype(F32)
+        return select.astype(BF16)
+
+    select_halo = selection(first - HALO, HALO)
+    select_own = selection(first, rows)
     pieces = width // DK
     for t in range(3):
-        edge = dot(select, extended[t])
+        edge = dot(select_halo, halo[t]) + dot(select_own, qkv[t])
         for j in range(pieces):
             base = edge_base + (t * pieces + j) * 16
             res[base : base + 16, :] = edge[:, j * DK : (j + 1) * DK].astype(BF16)
@@ -352,17 +388,40 @@
     for cp in ns_copies:
         cp.wait_recv()
     out_rows = blk * 2
-    proj_copies = []
-    for o in range(1, wins):
-        pw = lax.rem(w + o, wins)
+    cols = wq.shape[1] // 2
+    wy, wx = w // 2, lax.rem(w, 2)
+    side, across, far = wy * 2 + (1 - wx), (1 - wy) * 2 + wx, 3 - w
+
+    def project(pw):
         block = gathered[pl.ds(pl.multiple_of(pw * out_rows, out_rows), out_rows), :]
-        proj_send[o] = dot(block, wq[...]).astype(BF16)
-        cp = remote(
-            proj_send.at[o], proj_recv.at[o], proj_send_sem.at[o], proj_recv_sem.at[o], {"win": pw}
-        )
-        cp.start()
-        proj_copies.append(cp)
-    own = dot(gathered[pl.ds(pl.multiple_of(w * out_rows, out_rows), out_rows), :], wq[...])
+        return dot(block, wq[...])
+
+    def proj_copy(i, pw):
+        return remote(
+            proj_send.at[i], proj_recv.at[i], proj_send_sem.at[i], proj_recv_sem.at[i], {"win": pw}
+        )
+
+    proj_copies = [proj_copy(i, pw) for i, pw in enumerate((side, across) * 2 + (across, side))]
+    term = project(far).astype(BF16)
+    proj_send[0] = term[:, :cols]
+    proj_copies[0].start()
+    proj_send[1] = term[:, cols:]
+    proj_copies[1].start()
+    term = project(side)
+    proj_send[2] = term[:, :cols].astype(BF16)
+    proj_copies[2].start()
+    side_term = term[:, cols:]
+    term = project(across)
+    proj_send[3] = term[:, cols:].astype(BF16)
+    proj_copies[3].start()
+    across_term = term[:, :cols]
+    own = project(w)
+    proj_copies[0].wait_recv()
+    proj_send[4] = (across_term + proj_recv[0].astype(F32)).astype(BF16)
+    proj_copies[4].start()
+    proj_copies[1].wait_recv()
+    proj_send[5] = (side_term + proj_recv[1].astype(F32)).astype(BF16)
+    proj_copies[5].start()
 
     pl.when((k_idx == 2) & (k_idx > 1))(up_step)
     pl.when((k_idx == n - 3) & (k_idx < n - 2))(down_step)
@@ -373,13 +432,14 @@
     fs_out[...] = total_res[:edge_base]
     for t in range(3 * pieces):
         base = edge_base + t * 16
-        edge_out[:, t * DK : (t + 1) * DK] = total_res[base : base + 16].astype(BF16)
-
-    for cp in proj_copies:
+        edge_out[:, t * DK : (t + 1) * DK] = total_res[base : base + 16]
+
+    for cp in proj_copies[2:]:
         cp.wait_recv()
-    for o in range(1, wins):
-        own = own + proj_recv[o].astype(F32)
-    qkv_next[...] = own.astype(BF16)
+    for i, part in enumerate((slice(0, cols), slice(cols, 2 * cols))):
+        qkv_next[:, part] = (
+            own[:, part] + proj_recv[2 + i].astype(F32) + proj_recv[4 + i].astype(F32)
+        ).astype(BF16)
 
     wo_copy.wait_send()
     nh_copy.wait_send()
@@ -389,12 +449,37 @@
     @pl.when(not_last)
     def _():
         halo_copy.wait_send()
-        state_copy.wait_send()
+        for cp in state_copies:
+            cp.wait_send()
         up_copy.wait_send()
 
     @pl.when(not_first)
     def _():
         down_copy.wait_send()
+
+
+def place_results(
+    reqs, taps, width,
+    qkv_next, stream_out, states, edges,
+    qkv_next_out, stream_out_out, states_out, edges_out, sems,
+):
+    copies = [
+        pltpu.make_async_copy(src, dst, sems.at[i])
+        for i, (src, dst) in enumerate(
+            ((qkv_next, qkv_next_out), (stream_out, stream_out_out), (states, states_out))
+        )
+    ]
+    for cp in copies:
+        cp.start()
+    for r in range(reqs):
+        for i in range(taps):
+            row = r * taps + i
+            for t in range(3):
+                edges_out[r, i, t : t + 1, :] = edges[
+                    row : row + 1, t * width : (t + 1) * width
+                ].astype(BF16)
+    for cp in copies:
+        cp.wait()
 
 
 def solution(mesh):
@@ -416,7 +501,7 @@
                 jax.ShapeDtypeStruct((blk * 2, out_cols), BF16),
                 jax.ShapeDtypeStruct((blk, model), BF16),
                 jax.ShapeDtypeStruct((reqs * heads * DK, DK), F32),
-                jax.ShapeDtypeStruct((16, 3 * width), BF16),
+                jax.ShapeDtypeStruct((16, 3 * width), F32),
             ),
             in_specs=[pl.BlockSpec(memory_space=pltpu.SMEM)] + [vmem] * 6
             + [pl.BlockSpec(memory_space=pl.ANY)] * 2,
@@ -426,8 +511,8 @@
                 pltpu.VMEM((width, model), BF16),
                 pltpu.VMEM((width, model), BF16),
                 pltpu.VMEM((in_block, out_cols), BF16),
-                pltpu.VMEM((heads * DK, DK), BF16),
-                pltpu.VMEM((heads * DK, DK), BF16),
+                pltpu.VMEM((n // 2, heads * DK, DK), BF16),
+                pltpu.VMEM((n // 2, heads * DK, DK), BF16),
                 pltpu.VMEM((rows, width), BF16),
                 pltpu.VMEM((rows // 2, width), BF16),
                 pltpu.VMEM((rows // 2, width), BF16),
@@ -436,16 +521,16 @@
                 pltpu.VMEM((wins, blk, model), BF16),
                 pltpu.VMEM((blk, model), BF16),
                 pltpu.VMEM((rows, in_block), BF16),
-                pltpu.VMEM((wins, blk * 2, out_cols), BF16),
-                pltpu.VMEM((wins, blk * 2, out_cols), BF16),
+                pltpu.VMEM((6, blk * 2, out_cols // 2), BF16),
+                pltpu.VMEM((6, blk * 2, out_cols // 2), BF16),
                 pltpu.VMEM((res_rows, DK), BF16),
                 pltpu.VMEM((res_rows, DK), BF16),
                 pltpu.VMEM((res_rows, DK), BF16),
                 pltpu.VMEM((res_rows, DK), BF16),
                 pltpu.VMEM((res_rows, DK), BF16),
-                dma((2,)), dma((2,)), dma((2,)), dma((2,)), dma((2,)),
+                dma((2,)), dma((2,)), dma((2,)), dma((2, n // 2)), dma((2,)),
                 dma((wins,)), dma((wins,)), dma((group,)), dma((group,)),
-                dma((wins,)), dma((wins,)), dma((2,)), dma((2,)),
+                dma((6,)), dma((6,)), dma((2,)), dma((2,)),
             ],
             compiler_params=pltpu.CompilerParams(
                 collective_id=0, has_side_effects=True, vmem_limit_bytes=56 * 1024 * 1024
@@ -458,14 +543,19 @@
             lengths, jnp.transpose(qkv_in, (1, 0, 2)), conv_w, beta_logits,
             out_gain.reshape(1, DK), hidden_in, norm_gain.reshape(1, model), w_out, w_qkv,
         )
-        projected, stream, states, edges = results
         taps = CONV - 1
-        return (
-            projected,
-            stream,
-            states.reshape(reqs, heads, DK, DK),
-            edges[: reqs * taps].reshape(reqs, taps, 3, width),
-        )
+        place = pl.BlockSpec(memory_space=pl.ANY)
+        projected, stream, states, edges = pl.pallas_call(
+            functools.partial(place_results, reqs, taps, width),
+            out_shape=tuple(jax.ShapeDtypeStruct(x.shape, x.dtype) for x in results[:3])
+            + (jax.ShapeDtypeStruct((reqs, taps, 3, width), BF16),),
+            in_specs=[place] * 3 + [vmem],
+            out_specs=(place,) * 3 + (vmem,),
+            scratch_shapes=[dma((3,))],
+            compiler_params=pltpu.CompilerParams(vmem_limit_bytes=60 * 1024 * 1024),
+            name="place_results",
+        )(*results)
+        return projected, stream, states.reshape(reqs, heads, DK, DK), edges
 
     return jax.shard_map(
         body,

time: 62.7 us -> 83.5 us (1.33)
  Pallas kernels: 55.1 us -> 81.2 us
  local copies, waits for them, and re-layouts: 6.57 us -> 1.35 us
    pallas_call x0 -> x1, Pallas kernels: none -> 34.3 us  [body(): pl.pallas_call(functools.partial(place_results, reqs, taps, width), out_s...]
    pallas_call x1, Pallas kernels: 55.1 us -> 46.9 us  [body(): pl.pallas_call(functools.partial(kernel, n, wins, reqs), out_shape=(jax.S...]
    unnamed x4 -> x1, local copies, waits for them, and re-layouts: 5.82 us -> 1.35 us
where the time goes in v2:
time: 83.5 us; the launch traced here: 83.2 us
  Pallas kernels  81.2 us (97%)
  local copies, waits for them, and re-layouts  1.35 us (2%)
    pallas_call x1, Pallas kernels, body(): pl.pallas_call(functools.partial(kernel, n, wins, reqs), out_shape=(jax.S...  46.9 us
    pallas_call x1, Pallas kernels, body(): pl.pallas_call(functools.partial(place_results, reqs, taps, width), out_s...  34.3 us

profile of v2, /device:TPU:24, one launch (start us, length us, event | category | flops | bytes accessed | tf_op | source)
XLA Modules:
  0.0 83.2 jit_solution(14063785491282304944)
XLA Ops:
  0.6 46.9 %delta_sublayer.1 = (bf16[64,3072]{1,0:T(8,128)(2,1)}, bf16[32,2048]{1,0:T(8,128)(2,1)}, f32[1024,128]{1,0:T(8,128)}, f32[16,768]{1,0:T(8,128)}) custom-call(s32[4]{0:T(128)} %lengths.1, bf16[3,256,256]{2,1,0:T(8,128)(2,1)} %bitcast.5, f32[3,4,256]{2,1,0:T(4,128)} %conv_w.1, f32[2,256]{1,0:T(2,128)} %beta.1, f32[1,128]{1,0:T(1,128)} %bitcast.7, ...), custom_call_target="tpu_custom_call" | custom-call | flops 4000000000 | bytes 8000000 | tf_op jit(solution)/shard_map/delta_sublayer/pallas_call | solution.py:498
  47.6 34.3 %place_results.1 = (bf16[64,3072]{1,0:T(8,128)(2,1)}, bf16[32,2048]{1,0:T(8,128)(2,1)}, f32[1024,128]{1,0:T(8,128)}, bf16[4,3,3,256]{3,2,1,0:T(4,128)(2,1)}) custom-call(bf16[64,3072]{1,0:T(8,128)(2,1)} %get-tuple-element.12.qkv_next, bf16[32,2048]{1,0:T(8,128)(2,1)} %get-tuple-element.13.stream_out, f32[1024,128]{1,0:T(8,128)} %get-tuple-element.14.states, ...), custom_call_target="tpu_custom_call" | custom-call | tf_op jit(solution)/shard_map/place_results/pallas_call | solution.py:548
  81.9 1.4 %copy.13 = bf16[4,3,3,256]{3,0,2,1:T(4,128)(2,1)} copy(bf16[4,3,3,256]{3,2,1,0:T(4,128)(2,1)} %get-tuple-element.23) | data formatting | bytes 36864

commit v3 on v2

--- a/solution.py
+++ b/solution.py
@@ -28,10 +28,24 @@
     return high, (x - high.astype(F32)).astype(BF16)
 
 
-def mm3(a, b, product=dot):
+def mm3(a, b):
     ah, al = split(a)
     bh, bl = split(b)
-    return product(ah, bh) + (product(ah, bl) + product(al, bh))
+    return dot(ah, bh) + (dot(ah, bl) + dot(al, bh))
+
+
+def mm1(a, b):
+    return dot(a.astype(BF16), b.astype(BF16))
+
+
+def mm_left(a, b):
+    high, low = split(a)
+    return dot(high, b) + dot(low, b)
+
+
+def mm_right(a, b):
+    high, low = split(b)
+    return dot(a, high) + dot(a, low)
 
 
 def kernel(
@@ -189,19 +203,27 @@
             )
         activated.append(jnp.concatenate([silu(pre), mains[t]], axis=0))
 
-    def unit(x):
-        return x * lax.rsqrt(jnp.sum(x * x, axis=-1, keepdims=True) + 1e-6)
-
-    q, k, v, kt, a_full, scores = [], [], [], [], [], []
+    def norm_factor(x, axis):
+        return lax.rsqrt(jnp.sum(x * x, axis=axis, keepdims=True) + 1e-6)
+
+    q, k, v, kt, k_col, a_full, scores = [], [], [], [], [], [], []
     for h in range(heads):
         cols = slice(h * DK, (h + 1) * DK)
-        q.append(unit(activated[0][:, cols]))
-        k.append(unit(activated[1][:, cols]))
+        q_raw, k_raw = activated[0][:, cols], activated[1][:, cols]
+        q_col = norm_factor(q_raw, 1)
+        k_col.append(norm_factor(k_raw, 1))
+        kt_raw = jnp.transpose(k_raw)
+        k_row = norm_factor(kt_raw, 0)
+        q.append(q_raw * q_col)
+        k.append(k_raw * k_col[h])
         v.append(activated[2][:, cols])
-        kt.append(jnp.transpose(k[h]))
-        gram = mm3(k[h], k[h], dot_t)
-        a_full.append(jnp.where(strict, strength[h] * gram, 0.0))
-        scores.append(jnp.where(causal, mm3(q[h], k[h], dot_t), 0.0))
+        kt.append(kt_raw)
+        k_half = k_raw.astype(BF16)
+        gram = dot_t(k_half, k_half) * k_row
+        a_full.append(jnp.where(strict, (strength[h] * k_col[h]) * gram, 0.0))
+        scores.append(
+            jnp.where(causal, q_col * (dot_t(q_raw.astype(BF16), k_half) * k_row), 0.0)
+        )
 
     diag = []
     for h in range(heads):
@@ -219,18 +241,18 @@
         if level == 0:
             inverse = [eye_half - x for x in lower]
         else:
-            ys = [mm3(x, z) for x, z in zip(lower, inverse)]
-            inverse = [z - mm3(z, y) for z, y in zip(inverse, ys)]
+            ys = [mm1(x, z) for x, z in zip(lower, inverse)]
+            inverse = [z - mm1(z, y) for z, y in zip(inverse, ys)]
         level += 1
 
     solved, out_local, q_link, trans, write = [], [], [], [], []
     for h in range(heads):
         rhs = jnp.concatenate([strength[h] * v[h], (strength[h] * coupled) * k[h]], axis=1)
         top = mm3(inverse[2 * h], rhs[:half])
-        low = mm3(inverse[2 * h + 1], rhs[half:] - mm3(a_full[h][half:, :half], top))
+        low = mm3(inverse[2 * h + 1], rhs[half:] - mm1(a_full[h][half:, :half], top))
         solved.append(jnp.concatenate([top, low], axis=0))
     for h in range(heads):
-        m = mm3(kt[h] * in_last, solved[h])
+        m = mm_right((kt[h] * in_last).astype(BF16), k_col[h] * solved[h])
         write.append(m[:, :DK])
         trans.append(last_link * (eye_keys - m[:, DK:]))
 
@@ -246,51 +268,35 @@
             hr = slice(h * DK, (h + 1) * DK)
             state = write[h]
             if i > 0:
-                state = state + mm3(trans[h], state_recv[i - 1, hr, :].astype(F32))
+                state = state + mm_left(trans[h], state_recv[i - 1, hr, :])
             state_send[i, hr, :] = state.astype(BF16)
         pl.when(not_last)(state_copies[i].start)
         if i == 0:
-            local = [mm3(scores[h], solved[h]) for h in range(heads)]
-            links = [
-                jnp.concatenate([coupled * q[h] - local[h][:, DK:], solved[h][:, DK:]], axis=0)
-                for h in range(heads)
-            ]
+            local = [mm1(scores[h], solved[h]) for h in range(heads)]
+            links = [coupled * q[h] - local[h][:, DK:] for h in range(heads)]
     pl.when(not_first)(state_copies[steps - 1].wait_recv)
     state_in = [
-        state_recv[steps - 1, h * DK : (h + 1) * DK, :].astype(F32) for h in range(heads)
+        state_recv[steps - 1, h * DK : (h + 1) * DK, :] for h in range(heads)
     ]
 
     corrected = []
     for h in range(heads):
-        s = local[h]
-        applied = mm3(links[h], state_in[h])
-        att = s[:, :DK] + applied[:rows]
-        corrected.append(solved[h][:, :DK] - applied[rows:])
+        att = local[h][:, :DK] + dot(links[h].astype(BF16), state_in[h])
+        corrected.append(k_col[h] * (solved[h][:, :DK] - mm_left(solved[h][:, DK:], state_in[h])))
         scale = lax.rsqrt(jnp.mean(att * att, axis=-1, keepdims=True) + 1e-5)
         nh[:, h * DK : (h + 1) * DK] = (att * scale * out_gain[...]).astype(BF16)
 
-    for o in range(wins):
-        start = pl.multiple_of((2 * o + 1 - c) * blk, blk)
-        nh_send[o * blk : (o + 1) * blk, :] = nh[pl.ds(start, blk), :]
+    wy, wx = w // 2, lax.rem(w, 2)
+    side, across, far = wy * 2 + (1 - wx), (1 - wy) * 2 + wx, 3 - w
+    order = (w, side, across, far)
+
+    def rows_for(pw, pc):
+        return nh[pl.ds(pl.multiple_of((2 * pw + pc) * blk, blk), blk), :]
+
+    for i, pw in enumerate(order):
+        nh_send[i * blk : (i + 1) * blk, :] = rows_for(pw, 1 - c)
     nh_copy = remote(nh_send, nh_recv, nh_sem.at[0], nh_sem.at[1], sib)
     nh_copy.start()
-    own_rows = jnp.concatenate(
-        [nh[pl.ds(pl.multiple_of((2 * o + c) * blk, blk), blk), :] for o in range(wins)], axis=0
-    )
-    copy_wo.wait()
-    wo_copy.wait_recv()
-    part_keep[...] = dot(own_rows, wo_own[...])
-    nh_copy.wait_recv()
-    part_keep[...] = part_keep[...] + dot(nh_recv[...], wo_sib[...])
-    part_copies = []
-    for o in range(1, wins):
-        pw = lax.rem(w + o, wins)
-        part_send[o] = part_keep[pl.ds(pl.multiple_of(pw * blk, blk), blk), :].astype(BF16)
-        cp = remote(
-            part_send.at[o], part_recv.at[o], part_send_sem.at[o], part_recv_sem.at[o], {"win": pw}
-        )
-        cp.start()
-        part_copies.append(cp)
 
     for r in range(reqs):
         owned = (ends[r] - 1 >= first) & (ends[r] - 1 < first + rows)
@@ -300,7 +306,8 @@
         for h in range(heads):
             base = (r * heads + h) * DK
             res[base : base + DK, :] = (
-                mm3(kt[h] * member, corrected[h]) + carry * state_in[h]
+                mm_right((kt[h] * member).astype(BF16), corrected[h])
+                + carry * state_in[h].astype(F32)
             ).astype(BF16)
     edge_base = reqs * heads * DK
 
@@ -360,10 +367,58 @@
         down_send[...] = res[...]
         down_copy.start()
 
-    summed = hidden[...].astype(F32) + part_keep[pl.ds(pl.multiple_of(w * blk, blk), blk), :]
-    for o in range(1, wins):
-        part_copies[o - 1].wait_recv()
-        summed = summed + part_recv[o].astype(F32)
+    own_rows = jnp.concatenate([rows_for(pw, c) for pw in order], axis=0)
+    copy_wo.wait()
+    part_keep[...] = dot(own_rows, wo_own[...])
+    wo_copy.wait_recv()
+    nh_copy.wait_recv()
+
+    def win_copies(send, recv, send_sem, recv_sem):
+        return [
+            remote(send.at[i], recv.at[i], send_sem.at[i], recv_sem.at[i], {"win": pw})
+            for i, pw in enumerate((side, across) * 2 + (across, side))
+        ]
+
+    part_copies = win_copies(part_send, part_recv, part_send_sem, part_recv_sem)
+    model = hidden.shape[1]
+    part_cols = model // 2
+
+    def relay(copies, send, recv, cols, far_term, side_term, across_term, own_term):
+        term = far_term().astype(BF16)
+        send[0] = term[:, :cols]
+        copies[0].start()
+        send[1] = term[:, cols:]
+        copies[1].start()
+        term = side_term()
+        send[2] = term[:, :cols].astype(BF16)
+        copies[2].start()
+        side_rest = term[:, cols:]
+        term = across_term()
+        send[3] = term[:, cols:].astype(BF16)
+        copies[3].start()
+        across_rest = term[:, :cols]
+        own = own_term()
+        copies[0].wait_recv()
+        send[4] = (across_rest + recv[0].astype(F32)).astype(BF16)
+        copies[4].start()
+        copies[1].wait_recv()
+        send[5] = (side_rest + recv[1].astype(F32)).astype(BF16)
+        copies[5].start()
+        return own
+
+    part_all = part_keep[...] + dot(nh_recv[...], wo_sib[...])
+    part_terms = [part_all[i * blk : (i + 1) * blk] for i in range(wins)]
+    own_part = relay(
+        part_copies, part_send, part_recv, part_cols,
+        lambda: part_terms[3], lambda: part_terms[1], lambda: part_terms[2],
+        lambda: part_terms[0] + hidden[...].astype(F32),
+    )
+
+    for cp in part_copies[2:]:
+        cp.wait_recv()
+    summed = own_part + jnp.concatenate(
+        [part_recv[2 + i].astype(F32) + part_recv[4 + i].astype(F32) for i in range(2)], axis=1
+    )
     stream_out[...] = summed.astype(BF16)
     scale = lax.rsqrt(jnp.mean(summed * summed, axis=-1, keepdims=True) + 1e-5)
     ns[...] = (summed * scale * norm_gain[...]).astype(BF16)
@@ -389,39 +444,16 @@
         cp.wait_recv()
     out_rows = blk * 2
     cols = wq.shape[1] // 2
-    wy, wx = w // 2, lax.rem(w, 2)
-    side, across, far = wy * 2 + (1 - wx), (1 - wy) * 2 + wx, 3 - w
 
     def project(pw):
         block = gathered[pl.ds(pl.multiple_of(pw * out_rows, out_rows), out_rows), :]
         return dot(block, wq[...])
 
-    def proj_copy(i, pw):
-        return remote(
-            proj_send.at[i], proj_recv.at[i], proj_send_sem.at[i], proj_recv_sem.at[i], {"win": pw}
-        )
-
-    proj_copies = [proj_copy(i, pw) for i, pw in enumerate((side, across) * 2 + (across, side))]
-    term = project(far).astype(BF16)
-    proj_send[0] = term[:, :cols]
-    proj_copies[0].start()
-    proj_send[1] = term[:, cols:]
-    proj_copies[1].start()
-    term = project(side)
-    proj_send[2] = term[:, :cols].astype(BF16)
-    proj_copies[2].start()
-    side_term = term[:, cols:]
-    term = project(across)
-    proj_send[3] = term[:, cols:].astype(BF16)
-    proj_copies[3].start()
-    across_term = term[:, :cols]
-    own = project(w)
-    proj_copies[0].wait_recv()
-    proj_send[4] = (across_term + proj_recv[0].astype(F32)).astype(BF16)
-    proj_copies[4].start()
-    proj_copies[1].wait_recv()
-    proj_send[5] = (side_term + proj_recv[1].astype(F32)).astype(BF16)
-    proj_copies[5].start()
+    proj_copies = win_copies(proj_send, proj_recv, proj_send_sem, proj_recv_sem)
+    own = relay(
+        proj_copies, proj_send, proj_recv, cols,
+        lambda: project(far), lambda: project(side), lambda: project(across), lambda: project(w),
+    )
 
     pl.when((k_idx == 2) & (k_idx > 1))(up_step)
     pl.when((k_idx == n - 3) & (k_idx < n - 2))(down_step)
@@ -461,24 +493,34 @@
 def place_results(
     reqs, taps, width,
     qkv_next, stream_out, states, edges,
-    qkv_next_out, stream_out_out, states_out, edges_out, sems,
+    qkv_next_out, stream_out_out, states_out, edges_out,
+    qkv_held, stream_held, states_held, edges_held, sems,
 ):
-    copies = [
+    held = (qkv_held, stream_held, states_held)
+    arrive = [
         pltpu.make_async_copy(src, dst, sems.at[i])
+        for i, (src, dst) in enumerate(zip((qkv_next, stream_out, states), held))
+    ]
+    leave = [
+        pltpu.make_async_copy(src, dst, sems.at[3 + i])
         for i, (src, dst) in enumerate(
-            ((qkv_next, qkv_next_out), (stream_out, stream_out_out), (states, states_out))
+            zip(held + (edges_held,), (qkv_next_out, stream_out_out, states_out, edges_out))
         )
     ]
-    for cp in copies:
+    for cp in arrive:
         cp.start()
     for r in range(reqs):
         for i in range(taps):
             row = r * taps + i
             for t in range(3):
-                edges_out[r, i, t : t + 1, :] = edges[
+                edges_held[r, i, t : t + 1, :] = edges[
                     row : row + 1, t * width : (t + 1) * width
                 ].astype(BF16)
-    for cp in copies:
+    leave[3].start()
+    for i in range(3):
+        arrive[i].wait()
+        leave[i].start()
+    for cp in leave:
         cp.wait()
 
 
@@ -517,8 +559,8 @@
                 pltpu.VMEM((rows // 2, width), BF16),
                 pltpu.VMEM((rows // 2, width), BF16),
                 pltpu.VMEM((rows // 2, model), F32),
-                pltpu.VMEM((wins, blk, model), BF16),
-                pltpu.VMEM((wins, blk, model), BF16),
+                pltpu.VMEM((6, blk, model // 2), BF16),
+                pltpu.VMEM((6, blk, model // 2), BF16),
                 pltpu.VMEM((blk, model), BF16),
                 pltpu.VMEM((rows, in_block), BF16),
                 pltpu.VMEM((6, blk * 2, out_cols // 2), BF16),
@@ -529,7 +571,7 @@
                 pltpu.VMEM((res_rows, DK), BF16),
                 pltpu.VMEM((res_rows, DK), BF16),
                 dma((2,)), dma((2,)), dma((2,)), dma((2, n // 2)), dma((2,)),
-                dma((wins,)), dma((wins,)), dma((group,)), dma((group,)),
+                dma((6,)), dma((6,)), dma((group,)), dma((group,)),
                 dma((6,)), dma((6,)), dma((2,)), dma((2,)),
             ],
             compiler_params=pltpu.CompilerParams(
@@ -550,8 +592,9 @@
             out_shape=tuple(jax.ShapeDtypeStruct(x.shape, x.dtype) for x in results[:3])
             + (jax.ShapeDtypeStruct((reqs, taps, 3, width), BF16),),
             in_specs=[place] * 3 + [vmem],
-            out_specs=(place,) * 3 + (vmem,),
-            scratch_shapes=[dma((3,))],
+            out_specs=(place,) * 4,
+            scratch_shapes=[pltpu.VMEM(x.shape, x.dtype) for x in results[:3]]
+            + [pltpu.VMEM((reqs, taps, 3, width), BF16), dma((7,))],
             compiler_params=pltpu.CompilerParams(vmem_limit_bytes=60 * 1024 * 1024),
             name="place_results",
         )(*results)

time: 83.5 us -> 49.6 us (0.59)
  Pallas kernels: 81.2 us -> 47.4 us
    pallas_call x1, Pallas kernels: 34.3 us -> 2.89 us  [body(): pl.pallas_call(functools.partial(place_results, reqs, taps, width), out_s...]
    pallas_call x1, Pallas kernels: 46.9 us -> 44.5 us  [body(): pl.pallas_call(functools.partial(kernel, n, wins, reqs), out_shape=(jax.S...]
where the time goes in v3:
time: 49.6 us; the launch traced here: 49.4 us
  Pallas kernels  47.4 us (96%)
  local copies, waits for them, and re-layouts  1.35 us (3%)
  between operations  0.65 us (1%)
    pallas_call x1, Pallas kernels, body(): pl.pallas_call(functools.partial(kernel, n, wins, reqs), out_shape=(jax.S...  44.5 us
    pallas_call x1, Pallas kernels, body(): pl.pallas_call(functools.partial(place_results, reqs, taps, width), out_s...  2.89 us
    unnamed x1, local copies, waits for them, and re-layouts  1.35 us

profile of v3, /device:TPU:24, one launch (start us, length us, event | category | flops | bytes accessed | tf_op | source)
XLA Modules:
  0.0 49.4 jit_solution(659056820343842166)
XLA Ops:
  0.6 44.5 %delta_sublayer.1 = (bf16[64,3072]{1,0:T(8,128)(2,1)}, bf16[32,2048]{1,0:T(8,128)(2,1)}, f32[1024,128]{1,0:T(8,128)}, f32[16,768]{1,0:T(8,128)}) custom-call(s32[4]{0:T(128)} %lengths.1, bf16[3,256,256]{2,1,0:T(8,128)(2,1)} %bitcast.5, f32[3,4,256]{2,1,0:T(4,128)} %conv_w.1, f32[2,256]{1,0:T(2,128)} %beta.1, f32[1,128]{1,0:T(1,128)} %bitcast.7, ...), custom_call_target="tpu_custom_call" | custom-call | flops 4000000000 | bytes 8000000 | tf_op jit(solution)/shard_map/delta_sublayer/pallas_call | solution.py:540
  45.1 2.9 %place_results.1 = (bf16[64,3072]{1,0:T(8,128)(2,1)}, bf16[32,2048]{1,0:T(8,128)(2,1)}, f32[1024,128]{1,0:T(8,128)}, bf16[4,3,3,256]{3,2,1,0:T(4,128)(2,1)}) custom-call(bf16[64,3072]{1,0:T(8,128)(2,1)} %get-tuple-element.12.qkv_next, bf16[32,2048]{1,0:T(8,128)(2,1)} %get-tuple-element.13.stream_out, f32[1024,128]{1,0:T(8,128)} %get-tuple-element.14.states, ...), custom_call_target="tpu_custom_call" | custom-call | tf_op jit(solution)/shard_map/place_results/pallas_call | solution.py:590
  48.0 1.4 %copy.13 = bf16[4,3,3,256]{3,0,2,1:T(4,128)(2,1)} copy(bf16[4,3,3,256]{3,2,1,0:T(4,128)(2,1)} %get-tuple-element.23) | data formatting | bytes 36864

commit v4 on v3

--- a/solution.py
+++ b/solution.py
@@ -51,8 +51,8 @@
 def kernel(
     n, wins, reqs,
     lengths, qkv, conv_w, beta, out_gain, hidden, norm_gain, w_out, w_qkv,
-    qkv_next, stream_out, fs_out, edge_out,
-    halo, wo_own, wo_sib, wq, state_send, state_recv, nh, nh_send, nh_recv,
+    qkv_next, stream_hbm, fs_hbm, edge_out,
+    stream_out, fs_out, halo, wo_own, wo_sib, wq, state_send, state_recv, nh, nh_send, nh_recv,
     part_keep, part_send, part_recv, ns, gathered, proj_send, proj_recv,
     res, up_send, up_recv, down_send, down_recv,
     local_sem, halo_sem, wo_sem, state_sem, nh_sem, part_send_sem, part_recv_sem,
@@ -101,26 +101,6 @@
     copy_wq = pltpu.make_async_copy(w_qkv, wq, local_sem.at[1])
     copy_wo.start()
     copy_wq.start()
-    pl.semaphore_wait(
-        barrier, group - 1 + not_first.astype(jnp.int32) + not_last.astype(jnp.int32)
-    )
-
-    halo_copy = remote(
-        qkv.at[:, pl.ds(rows - HALO, HALO), :], halo, halo_sem.at[0], halo_sem.at[1], above
-    )
-
-    @pl.when(not_last)
-    def _():
-        halo_copy.start()
-
-    wo_copy = remote(w_out, wo_sib, wo_sem.at[0], wo_sem.at[1], sib)
-    wo_copy.start()
-
-    @pl.when(jnp.logical_not(not_first))
-    def _():
-        halo[...] = jnp.zeros_like(halo)
-        state_recv[...] = jnp.zeros_like(state_recv)
-
     ends = []
     total = jnp.int32(0)
     for r in range(reqs):
@@ -174,7 +154,7 @@
 
     pres = []
     mains = []
-    for t in range(3):
+    def convolve(t):
         wide = qkv[t].astype(F32)
         pre = tap(t, 0) * wide
         for back in range(1, CONV):
@@ -183,6 +163,29 @@
         pres.append(pre[:8])
         mains.append(silu(pre)[8:])
 
+    convolve(0)
+    pl.semaphore_wait(
+        barrier, group - 1 + not_first.astype(jnp.int32) + not_last.astype(jnp.int32)
+    )
+
+    halo_copy = remote(
+        qkv.at[:, pl.ds(rows - HALO, HALO), :], halo, halo_sem.at[0], halo_sem.at[1], above
+    )
+
+    @pl.when(not_last)
+    def _():
+        halo_copy.start()
+
+    wo_copy = remote(w_out, wo_sib, wo_sem.at[0], wo_sem.at[1], sib)
+    wo_copy.start()
+
+    @pl.when(jnp.logical_not(not_first))
+    def _():
+        halo[...] = jnp.zeros_like(halo)
+        state_recv[...] = jnp.zeros_like(state_recv)
+
+    convolve(1)
+    convolve(2)
     strength = []
     for h in range(heads):
         b_row = 1.0 / (1.0 + jnp.exp(-beta[h : h + 1, :]))
@@ -258,29 +261,33 @@
 
     steps = n // 2
     state_copies = [
-        remote(state_send.at[i], state_recv.at[i], state_sem.at[0, i], state_sem.at[1, i], above)
+        [
+            remote(
+                state_send.at[i, pl.ds(h * DK, DK)], state_recv.at[i, pl.ds(h * DK, DK)],
+                state_sem.at[0, i * heads + h], state_sem.at[1, i * heads + h], above,
+            )
+            for h in range(heads)
+        ]
         for i in range(steps)
     ]
     for i in range(steps):
-        if i > 0:
-            pl.when(not_first)(state_copies[i - 1].wait_recv)
         for h in range(heads):
             hr = slice(h * DK, (h + 1) * DK)
             state = write[h]
             if i > 0:
+                pl.when(not_first)(state_copies[i - 1][h].wait_recv)
                 state = state + mm_left(trans[h], state_recv[i - 1, hr, :])
             state_send[i, hr, :] = state.astype(BF16)
-        pl.when(not_last)(state_copies[i].start)
+            pl.when(not_last)(state_copies[i][h].start)
         if i == 0:
             local = [mm1(scores[h], solved[h]) for h in range(heads)]
             links = [coupled * q[h] - local[h][:, DK:] for h in range(heads)]
-    pl.when(not_first)(state_copies[steps - 1].wait_recv)
-    state_in = [
-        state_recv[steps - 1, h * DK : (h + 1) * DK, :] for h in range(heads)
-    ]
+    state_in = []
 
     corrected = []
     for h in range(heads):
+        pl.when(not_first)(state_copies[steps - 1][h].wait_recv)
+        state_in.append(state_recv[steps - 1, h * DK : (h + 1) * DK, :])
         att = local[h][:, :DK] + dot(links[h].astype(BF16), state_in[h])
         corrected.append(k_col[h] * (solved[h][:, :DK] - mm_left(solved[h][:, DK:], state_in[h])))
         scale = lax.rsqrt(jnp.mean(att * att, axis=-1, keepdims=True) + 1e-5)
@@ -320,7 +327,7 @@
             owned = (ends[r] - 1 >= first) & (ends[r] - 1 < first + rows)
             for i in range(CONV - 1):
                 hit = (
-                    (sel_row == r * (CONV - 1) + i)
+                    (sel_row == i * reqs + r)
                     & (sel_pos == ends[r] - (CONV - 1) + i)
                     & (sel_seg == r)
                 )
@@ -420,39 +427,51 @@
         [part_recv[2 + i].astype(F32) + part_recv[4 + i].astype(F32) for i in range(2)], axis=1
     )
     stream_out[...] = summed.astype(BF16)
+    stream_copy = pltpu.make_async_copy(stream_out, stream_hbm, local_sem.at[2])
+    stream_copy.start()
     scale = lax.rsqrt(jnp.mean(summed * summed, axis=-1, keepdims=True) + 1e-5)
     ns[...] = (summed * scale * norm_gain[...]).astype(BF16)
     in_block = wq.shape[0]
     my_rows = pl.ds(pl.multiple_of(me * blk, blk), blk)
     ns_copies = []
-    for o in range(1, group):
-        pw, pc = peer(o)
-        cp = remote(
-            ns.at[:, pl.ds(pl.multiple_of(pw * in_block, in_block), in_block)],
-            gathered.at[my_rows, :],
-            ns_send_sem.at[o], ns_recv_sem.at[o], {"win": pw, "wout": pc},
-        )
-        cp.start()
-        ns_copies.append(cp)
+    for pw in (far, side, across):
+        for pc in (c, 1 - c):
+            i = len(ns_copies)
+            cp = remote(
+                ns.at[:, pl.ds(pl.multiple_of(pw * in_block, in_block), in_block)],
+                gathered.at[my_rows, :],
+                ns_send_sem.at[i], ns_recv_sem.at[i], {"win": pw, "wout": pc},
+            )
+            cp.start()
+            ns_copies.append(cp)
+    last = len(ns_copies)
+    cp = remote(
+        ns.at[:, pl.ds(pl.multiple_of(w * in_block, in_block), in_block)],
+        gathered.at[my_rows, :],
+        ns_send_sem.at[last], ns_recv_sem.at[last], sib,
+    )
+    cp.start()
+    ns_copies.append(cp)
     gathered[my_rows, :] = ns[:, pl.ds(pl.multiple_of(w * in_block, in_block), in_block)]
 
     pl.when(k_idx == 1)(up_step)
     pl.when(k_idx == n - 2)(down_step)
 
     copy_wq.wait()
-    for cp in ns_copies:
-        cp.wait_recv()
     out_rows = blk * 2
     cols = wq.shape[1] // 2
 
-    def project(pw):
+    def project(pw, arriving):
+        for cp in arriving:
+            cp.wait_recv()
         block = gathered[pl.ds(pl.multiple_of(pw * out_rows, out_rows), out_rows), :]
         return dot(block, wq[...])
 
     proj_copies = win_copies(proj_send, proj_recv, proj_send_sem, proj_recv_sem)
     own = relay(
         proj_copies, proj_send, proj_recv, cols,
-        lambda: project(far), lambda: project(side), lambda: project(across), lambda: project(w),
+        lambda: project(far, ns_copies[0:2]), lambda: project(side, ns_copies[2:4]),
+        lambda: project(across, ns_copies[4:6]), lambda: project(w, ns_copies[6:]),
     )
 
     pl.when((k_idx == 2) & (k_idx > 1))(up_step)
@@ -461,7 +480,9 @@
     pl.when(k_idx < n - 3)(down_step)
 
     total_res = res[...].astype(F32) + up_recv[...].astype(F32) + down_recv[...].astype(F32)
-    fs_out[...] = total_res[:edge_base]
+    fs_out[...] = total_res[:edge_base].astype(BF16)
+    fs_copy = pltpu.make_async_copy(fs_out, fs_hbm, local_sem.at[3])
+    fs_copy.start()
     for t in range(3 * pieces):
         base = edge_base + t * 16
         edge_out[:, t * DK : (t + 1) * DK] = total_res[base : base + 16]
@@ -473,6 +494,8 @@
             own[:, part] + proj_recv[2 + i].astype(F32) + proj_recv[4 + i].astype(F32)
         ).astype(BF16)
 
+    stream_copy.wait()
+    fs_copy.wait()
     wo_copy.wait_send()
     nh_copy.wait_send()
     for cp in part_copies + ns_copies + proj_copies:
@@ -481,7 +504,7 @@
     @pl.when(not_last)
     def _():
         halo_copy.wait_send()
-        for cp in state_copies:
+        for cp in [x for pair in state_copies for x in pair]:
             cp.wait_send()
         up_copy.wait_send()
 
@@ -494,7 +517,7 @@
     reqs, taps, width,
     qkv_next, stream_out, states, edges,
     qkv_next_out, stream_out_out, states_out, edges_out,
-    qkv_held, stream_held, states_held, edges_held, sems,
+    qkv_held, stream_held, states_held, states_wide, edges_held, sems,
 ):
     held = (qkv_held, stream_held, states_held)
     arrive = [
@@ -504,20 +527,21 @@
     leave = [
         pltpu.make_async_copy(src, dst, sems.at[3 + i])
         for i, (src, dst) in enumerate(
-            zip(held + (edges_held,), (qkv_next_out, stream_out_out, states_out, edges_out))
+            zip((qkv_held, stream_held, states_wide, edges_held), (qkv_next_out, stream_out_out, states_out, edges_out))
         )
     ]
-    for cp in arrive:
-        cp.start()
-    for r in range(reqs):
-        for i in range(taps):
-            row = r * taps + i
-            for t in range(3):
-                edges_held[r, i, t : t + 1, :] = edges[
-                    row : row + 1, t * width : (t + 1) * width
-                ].astype(BF16)
+    for i in (2, 0, 1):
+        arrive[i].start()
+    for i in range(taps):
+        for t in range(3):
+            edges_held[i, t] = edges[
+                i * reqs : (i + 1) * reqs, t * width : (t + 1) * width
+            ].astype(BF16)
     leave[3].start()
-    for i in range(3):
+    arrive[2].wait()
+    states_wide[...] = states_held[...].astype(F32)
+    leave[2].start()
+    for i in range(2):
         arrive[i].wait()
         leave[i].start()
     for cp in leave:
@@ -536,19 +560,22 @@
         group = wins * 2
         res_rows = reqs * heads * DK + 16 * 3 * (width // DK)
         vmem = pl.BlockSpec(memory_space=pltpu.VMEM)
+        place = pl.BlockSpec(memory_space=pl.ANY)
         dma = pltpu.SemaphoreType.DMA
         results = pl.pallas_call(
             functools.partial(kernel, n, wins, reqs),
             out_shape=(
                 jax.ShapeDtypeStruct((blk * 2, out_cols), BF16),
                 jax.ShapeDtypeStruct((blk, model), BF16),
-                jax.ShapeDtypeStruct((reqs * heads * DK, DK), F32),
+                jax.ShapeDtypeStruct((reqs * heads * DK, DK), BF16),
                 jax.ShapeDtypeStruct((16, 3 * width), F32),
             ),
             in_specs=[pl.BlockSpec(memory_space=pltpu.SMEM)] + [vmem] * 6
             + [pl.BlockSpec(memory_space=pl.ANY)] * 2,
-            out_specs=(vmem,) * 4,
+            out_specs=(vmem, place, place, vmem),
             scratch_shapes=[
+                pltpu.VMEM((blk, model), BF16),
+                pltpu.VMEM((reqs * heads * DK, DK), BF16),
                 pltpu.VMEM((3, HALO, width), BF16),
                 pltpu.VMEM((width, model), BF16),
                 pltpu.VMEM((width, model), BF16),
@@ -570,7 +597,7 @@
                 pltpu.VMEM((res_rows, DK), BF16),
                 pltpu.VMEM((res_rows, DK), BF16),
                 pltpu.VMEM((res_rows, DK), BF16),
-                dma((2,)), dma((2,)), dma((2,)), dma((2, n // 2)), dma((2,)),
+                dma((4,)), dma((2,)), dma((2,)), dma((2, n // 2 * heads)), dma((2,)),
                 dma((6,)), dma((6,)), dma((group,)), dma((group,)),
                 dma((6,)), dma((6,)), dma((2,)), dma((2,)),
             ],
@@ -586,19 +613,20 @@
             out_gain.reshape(1, DK), hidden_in, norm_gain.reshape(1, model), w_out, w_qkv,
         )
         taps = CONV - 1
-        place = pl.BlockSpec(memory_space=pl.ANY)
         projected, stream, states, edges = pl.pallas_call(
             functools.partial(place_results, reqs, taps, width),
-            out_shape=tuple(jax.ShapeDtypeStruct(x.shape, x.dtype) for x in results[:3])
-            + (jax.ShapeDtypeStruct((reqs, taps, 3, width), BF16),),
+            out_shape=tuple(jax.ShapeDtypeStruct(x.shape, x.dtype) for x in results[:2])
+            + (jax.ShapeDtypeStruct(results[2].shape, F32),)
+            + (jax.ShapeDtypeStruct((taps, 3, reqs, width), BF16),),
             in_specs=[place] * 3 + [vmem],
             out_specs=(place,) * 4,
             scratch_shapes=[pltpu.VMEM(x.shape, x.dtype) for x in results[:3]]
-            + [pltpu.VMEM((reqs, taps, 3, width), BF16), dma((7,))],
+            + [pltpu.VMEM(results[2].shape, F32)]
+            + [pltpu.VMEM((taps, 3, reqs, width), BF16), dma((7,))],
             compiler_params=pltpu.CompilerParams(vmem_limit_bytes=60 * 1024 * 1024),
             name="place_results",
         )(*results)
-        return projected, stream, states.reshape(reqs, heads, DK, DK), edges
+        return projected, stream, states.reshape(reqs, heads, DK, DK), jnp.transpose(edges, (2, 0, 1, 3))
 
     return jax.shard_map(
         body,

time: 49.6 us -> 46.6 us (0.940)
  Pallas kernels: 47.4 us -> 45.7 us
  local copies, waits for them, and re-layouts: 1.35 us -> 0 us
    pallas_call x1, Pallas kernels: 44.5 us -> 42.9 us  [body(): pl.pallas_call(functools.partial(kernel, n, wins, reqs), out_shape=(jax.S...]
    unnamed x1 -> x0, local copies, waits for them, and re-layouts: 1.35 us -> none
where the time goes in v4:
time: 46.6 us; the launch traced here: 46.4 us
  Pallas kernels  45.7 us (98%)
  between operations  0.64 us (1%)
    pallas_call x1, Pallas kernels, body(): pl.pallas_call(functools.partial(kernel, n, wins, reqs), out_shape=(jax.S...  42.9 us
    pallas_call x1, Pallas kernels, body(): pl.pallas_call(functools.partial(place_results, reqs, taps, width), out_s...  2.81 us

profile of v4, /device:TPU:24, one launch (start us, length us, event | category | flops | bytes accessed | tf_op | source)
XLA Modules:
  0.0 46.4 jit_solution(5492325168393627725)
XLA Ops:
  0.6 42.9 %delta_sublayer.1 = (bf16[64,3072]{1,0:T(8,128)(2,1)}, bf16[32,2048]{1,0:T(8,128)(2,1)}, bf16[1024,128]{1,0:T(8,128)(2,1)}, f32[16,768]{1,0:T(8,128)}) custom-call(s32[4]{0:T(128)} %lengths.1, bf16[3,256,256]{2,1,0:T(8,128)(2,1)} %bitcast.6, f32[3,4,256]{2,1,0:T(4,128)} %conv_w.1, f32[2,256]{1,0:T(2,128)} %beta.1, f32[1,128]{1,0:T(1,128)} %bitcast.9, ...), custom_call_target="tpu_custom_call" | custom-call | flops 4000000000 | bytes 8000000 | tf_op jit(solution)/shard_map/delta_sublayer/pallas_call | solution.py:565
  43.6 2.8 %place_results.1 = (bf16[64,3072]{1,0:T(8,128)(2,1)}, bf16[32,2048]{1,0:T(8,128)(2,1)}, f32[1024,128]{1,0:T(8,128)}, bf16[3,3,4,256]{3,2,1,0:T(4,128)(2,1)}) custom-call(bf16[64,3072]{1,0:T(8,128)(2,1)} %get-tuple-element.12.qkv_next, bf16[32,2048]{1,0:T(8,128)(2,1)} %get-tuple-element.13.stream_out, bf16[1024,128]{1,0:T(8,128)(2,1)} %get-tuple-element.14.states, ...), custom_call_target="tpu_custom_call" | custom-call | tf_op jit(solution)/shard_map/place_results/pallas_call | solution.py:616

commit v5 on v4

--- a/solution.py
+++ b/solution.py
@@ -50,12 +50,12 @@
 
 def kernel(
     n, wins, reqs,
-    lengths, qkv, conv_w, beta, out_gain, hidden, norm_gain, w_out, w_qkv,
+    lengths, qkv_hbm, conv_w_hbm, beta_hbm, out_gain_hbm, hidden_hbm, norm_gain_hbm, w_out, w_qkv,
     qkv_next, stream_hbm, fs_hbm, edge_out,
-    stream_out, fs_out, halo, wo_own, wo_sib, wq, state_send, state_recv, nh, nh_send, nh_recv,
+    qkv, conv_w, beta, out_gain, hidden, norm_gain, stream_out, fs_out, halo, wo_own, wo_sib, wq, state_send, state_recv, nh, nh_send, nh_recv,
     part_keep, part_send, part_recv, ns, gathered, proj_send, proj_recv,
     res, up_send, up_recv, down_send, down_recv,
-    local_sem, halo_sem, wo_sem, state_sem, nh_sem, part_send_sem, part_recv_sem,
+    local_sem, load_sem, halo_sem, wo_sem, state_sem, nh_sem, part_send_sem, part_recv_sem,
     ns_send_sem, ns_recv_sem, proj_send_sem, proj_recv_sem, up_sem, down_sem,
 ):
     rows = qkv.shape[1]
@@ -97,6 +97,15 @@
     def _():
         pl.semaphore_signal(barrier, inc=1, device_id=above, device_id_type=MESH)
 
+    loads = [
+        pltpu.make_async_copy(src, dst, load_sem.at[i])
+        for i, (src, dst) in enumerate((
+            (qkv_hbm, qkv), (conv_w_hbm, conv_w), (beta_hbm, beta),
+            (out_gain_hbm, out_gain), (hidden_hbm, hidden), (norm_gain_hbm, norm_gain),
+        ))
+    ]
+    for cp in loads:
+        cp.start()
     copy_wo = pltpu.make_async_copy(w_out, wo_own, local_sem.at[0])
     copy_wq = pltpu.make_async_copy(w_qkv, wq, local_sem.at[1])
     copy_wo.start()
@@ -163,13 +172,15 @@
         pres.append(pre[:8])
         mains.append(silu(pre)[8:])
 
+    loads[0].wait()
+    loads[1].wait()
     convolve(0)
     pl.semaphore_wait(
         barrier, group - 1 + not_first.astype(jnp.int32) + not_last.astype(jnp.int32)
     )
 
     halo_copy = remote(
-        qkv.at[:, pl.ds(rows - HALO, HALO), :], halo, halo_sem.at[0], halo_sem.at[1], above
+        qkv_hbm.at[:, pl.ds(rows - HALO, HALO), :], halo, halo_sem.at[0], halo_sem.at[1], above
     )
 
     @pl.when(not_last)
@@ -186,6 +197,7 @@
 
     convolve(1)
     convolve(2)
+    loads[2].wait()
     strength = []
     for h in range(heads):
         b_row = 1.0 / (1.0 + jnp.exp(-beta[h : h + 1, :]))
@@ -284,6 +296,7 @@
             links = [coupled * q[h] - local[h][:, DK:] for h in range(heads)]
     state_in = []
 
+    loads[3].wait()
     corrected = []
     for h in range(heads):
         pl.when(not_first)(state_copies[steps - 1][h].wait_recv)
@@ -390,35 +403,34 @@
     model = hidden.shape[1]
     part_cols = model // 2
 
-    def relay(copies, send, recv, cols, far_term, side_term, across_term, own_term):
-        term = far_term().astype(BF16)
-        send[0] = term[:, :cols]
-        copies[0].start()
-        send[1] = term[:, cols:]
-        copies[1].start()
-        term = side_term()
-        send[2] = term[:, :cols].astype(BF16)
+    def relay(copies, send, recv, far_term, side_term, across_term, own_term):
+        for i in range(2):
+            send[i] = far_term(i).astype(BF16)
+            copies[i].start()
+        send[2] = side_term(0).astype(BF16)
         copies[2].start()
-        side_rest = term[:, cols:]
-        term = across_term()
-        send[3] = term[:, cols:].astype(BF16)
+        send[3] = across_term(1).astype(BF16)
         copies[3].start()
-        across_rest = term[:, :cols]
-        own = own_term()
+        across_rest = across_term(0)
+        side_rest = side_term(1)
         copies[0].wait_recv()
         send[4] = (across_rest + recv[0].astype(F32)).astype(BF16)
         copies[4].start()
         copies[1].wait_recv()
         send[5] = (side_rest + recv[1].astype(F32)).astype(BF16)
         copies[5].start()
-        return own
-
+        return own_term()
+
+    loads[4].wait()
+    loads[5].wait()
     part_all = part_keep[...] + dot(nh_recv[...], wo_sib[...])
-    part_terms = [part_all[i * blk : (i + 1) * blk] for i in range(wins)]
+
+    def part_term(i):
+        return lambda j: part_all[i * blk : (i + 1) * blk, j * part_cols : (j + 1) * part_cols]
+
     own_part = relay(
-        part_copies, part_send, part_recv, part_cols,
-        lambda: part_terms[3], lambda: part_terms[1], lambda: part_terms[2],
-        lambda: part_terms[0] + hidden[...].astype(F32),
+        part_copies, part_send, part_recv, part_term(3), part_term(1), part_term(2),
+        lambda: part_all[:blk] + hidden[...].astype(F32),
     )
 
     for cp in part_copies[2:]:
@@ -462,16 +474,22 @@
     cols = wq.shape[1] // 2
 
     def project(pw, arriving):
-        for cp in arriving:
-            cp.wait_recv()
-        block = gathered[pl.ds(pl.multiple_of(pw * out_rows, out_rows), out_rows), :]
-        return dot(block, wq[...])
+        block_rows = pl.ds(pl.multiple_of(pw * out_rows, out_rows), out_rows)
+        pending = list(arriving)
+
+        def term(j):
+            while pending:
+                pending.pop().wait_recv()
+            return dot(gathered[block_rows, :], wq[:, j * cols : (j + 1) * cols])
+
+        return term
 
     proj_copies = win_copies(proj_send, proj_recv, proj_send_sem, proj_recv_sem)
+    own_term = project(w, ns_copies[6:])
     own = relay(
-        proj_copies, proj_send, proj_recv, cols,
-        lambda: project(far, ns_copies[0:2]), lambda: project(side, ns_copies[2:4]),
-        lambda: project(across, ns_copies[4:6]), lambda: project(w, ns_copies[6:]),
+        proj_copies, proj_send, proj_recv, project(far, ns_copies[0:2]),
+        project(side, ns_copies[2:4]), project(across, ns_copies[4:6]),
+        lambda: (own_term(0), own_term(1)),
     )
 
     pl.when((k_idx == 2) & (k_idx > 1))(up_step)
@@ -491,7 +509,7 @@
         cp.wait_recv()
     for i, part in enumerate((slice(0, cols), slice(cols, 2 * cols))):
         qkv_next[:, part] = (
-            own[:, part] + proj_recv[2 + i].astype(F32) + proj_recv[4 + i].astype(F32)
+            own[i] + proj_recv[2 + i].astype(F32) + proj_recv[4 + i].astype(F32)
         ).astype(BF16)
 
     stream_copy.wait()
@@ -570,10 +588,15 @@
                 jax.ShapeDtypeStruct((reqs * heads * DK, DK), BF16),
                 jax.ShapeDtypeStruct((16, 3 * width), F32),
             ),
-            in_specs=[pl.BlockSpec(memory_space=pltpu.SMEM)] + [vmem] * 6
-            + [pl.BlockSpec(memory_space=pl.ANY)] * 2,
+            in_specs=[pl.BlockSpec(memory_space=pltpu.SMEM)] + [place] * 8,
             out_specs=(vmem, place, place, vmem),
             scratch_shapes=[
+                pltpu.VMEM((3, rows, width), BF16),
+                pltpu.VMEM(conv_w.shape, F32),
+                pltpu.VMEM(beta_logits.shape, F32),
+                pltpu.VMEM((1, DK), F32),
+                pltpu.VMEM((blk, model), BF16),
+                pltpu.VMEM((1, model), F32),
                 pltpu.VMEM((blk, model), BF16),
                 pltpu.VMEM((reqs * heads * DK, DK), BF16),
                 pltpu.VMEM((3, HALO, width), BF16),
@@ -597,7 +620,7 @@
                 pltpu.VMEM((res_rows, DK), BF16),
                 pltpu.VMEM((res_rows, DK), BF16),
                 pltpu.VMEM((res_rows, DK), BF16),
-                dma((4,)), dma((2,)), dma((2,)), dma((2, n // 2 * heads)), dma((2,)),
+                dma((4,)), dma((6,)), dma((2,)), dma((2,)), dma((2, n // 2 * heads)), dma((2,)),
                 dma((6,)), dma((6,)), dma((group,)), dma((group,)),
                 dma((6,)), dma((6,)), dma((2,)), dma((2,)),
             ],

time: 46.6 us -> 47.1 us (1.011)
  Pallas kernels: 45.7 us -> 46.3 us
    pallas_call x1, Pallas kernels: 42.9 us -> 43.4 us  [body(): pl.pallas_call(functools.partial(kernel, n, wins, reqs), out_shape=(jax.S...]
where the time goes in v5:
time: 47.1 us; the launch traced here: 46.9 us
  Pallas kernels  46.3 us (98%)
  between operations  0.64 us (1%)
    pallas_call x1, Pallas kernels, body(): pl.pallas_call(functools.partial(kernel, n, wins, reqs), out_shape=(jax.S...  43.4 us
    pallas_call x1, Pallas kernels, body(): pl.pallas_call(functools.partial(place_results, reqs, taps, width), out_s...  2.81 us

profile of v5, /device:TPU:24, one launch (start us, length us, event | category | flops | bytes accessed | tf_op | source)
XLA Modules:
  0.0 46.9 jit_solution(8573520988430692416)
XLA Ops:
  0.6 43.4 %delta_sublayer.1 = (bf16[64,3072]{1,0:T(8,128)(2,1)}, bf16[32,2048]{1,0:T(8,128)(2,1)}, bf16[1024,128]{1,0:T(8,128)(2,1)}, f32[16,768]{1,0:T(8,128)}) custom-call(s32[4]{0:T(128)} %lengths.1, bf16[3,256,256]{2,1,0:T(8,128)(2,1)} %bitcast.6, f32[3,4,256]{2,1,0:T(4,128)} %conv_w_hbm.1, f32[2,256]{1,0:T(2,128)} %beta_hbm.1, f32[1,128]{1,0:T(1,128)} %bitcast.9, ...), custom_call_target="tpu_custom_call" | custom-call | flops 4000000000 | bytes 8000000 | tf_op jit(solution)/shard_map/delta_sublayer/pallas_call | solution.py:583
  44.1 2.8 %place_results.1 = (bf16[64,3072]{1,0:T(8,128)(2,1)}, bf16[32,2048]{1,0:T(8,128)(2,1)}, f32[1024,128]{1,0:T(8,128)}, bf16[3,3,4,256]{3,2,1,0:T(4,128)(2,1)}) custom-call(bf16[64,3072]{1,0:T(8,128)(2,1)} %get-tuple-element.12.qkv_next, bf16[32,2048]{1,0:T(8,128)(2,1)} %get-tuple-element.13.stream_out, bf16[1024,128]{1,0:T(8,128)(2,1)} %get-tuple-element.14.states, ...), custom_call_target="tpu_custom_call" | custom-call | tf_op jit(solution)/shard_map/place_results/pallas_call | solution.py:639

commit v6 on v4

--- a/solution.py
+++ b/solution.py
@@ -390,7 +390,7 @@
     model = hidden.shape[1]
     part_cols = model // 2
 
-    def relay(copies, send, recv, cols, far_term, side_term, across_term, own_term):
+    def relay(copies, send, recv, cols, far_term, side_term, across_term, own_term, between=None):
         term = far_term().astype(BF16)
         send[0] = term[:, :cols]
         copies[0].start()
@@ -404,6 +404,8 @@
         send[3] = term[:, cols:].astype(BF16)
         copies[3].start()
         across_rest = term[:, :cols]
+        if between is not None:
+            between()
         own = own_term()
         copies[0].wait_recv()
         send[4] = (across_rest + recv[0].astype(F32)).astype(BF16)
@@ -468,14 +470,17 @@
         return dot(block, wq[...])
 
     proj_copies = win_copies(proj_send, proj_recv, proj_send_sem, proj_recv_sem)
+    def second_step():
+        pl.when((k_idx == 2) & (k_idx > 1))(up_step)
+        pl.when((k_idx == n - 3) & (k_idx < n - 2))(down_step)
+
     own = relay(
         proj_copies, proj_send, proj_recv, cols,
         lambda: project(far, ns_copies[0:2]), lambda: project(side, ns_copies[2:4]),
         lambda: project(across, ns_copies[4:6]), lambda: project(w, ns_copies[6:]),
+        second_step,
     )
 
-    pl.when((k_idx == 2) & (k_idx > 1))(up_step)
-    pl.when((k_idx == n - 3) & (k_idx < n - 2))(down_step)
     pl.when(k_idx > 2)(up_step)
     pl.when(k_idx < n - 3)(down_step)
 

time: 46.6 us -> 46.6 us (level)
  no operation moved by 1% of the time
where the time goes in v6:
time: 46.6 us; the launch traced here: 46.4 us
  Pallas kernels  45.7 us (98%)
  between operations  0.64 us (1%)
    pallas_call x1, Pallas kernels, body(): pl.pallas_call(functools.partial(kernel, n, wins, reqs), out_shape=(jax.S...  42.9 us
    pallas_call x1, Pallas kernels, body(): pl.pallas_call(functools.partial(place_results, reqs, taps, width), out_s...  2.81 us

profile of v6, /device:TPU:24, one launch (start us, length us, event | category | flops | bytes accessed | tf_op | source)
XLA Modules:
  0.0 46.4 jit_solution(1437144676731400975)
XLA Ops:
  0.6 42.9 %delta_sublayer.1 = (bf16[64,3072]{1,0:T(8,128)(2,1)}, bf16[32,2048]{1,0:T(8,128)(2,1)}, bf16[1024,128]{1,0:T(8,128)(2,1)}, f32[16,768]{1,0:T(8,128)}) custom-call(s32[4]{0:T(128)} %lengths.1, bf16[3,256,256]{2,1,0:T(8,128)(2,1)} %bitcast.6, f32[3,4,256]{2,1,0:T(4,128)} %conv_w.1, f32[2,256]{1,0:T(2,128)} %beta.1, f32[1,128]{1,0:T(1,128)} %bitcast.9, ...), custom_call_target="tpu_custom_call" | custom-call | flops 4000000000 | bytes 8000000 | tf_op jit(solution)/shard_map/delta_sublayer/pallas_call | solution.py:570
  43.6 2.8 %place_results.1 = (bf16[64,3072]{1,0:T(8,128)(2,1)}, bf16[32,2048]{1,0:T(8,128)(2,1)}, f32[1024,128]{1,0:T(8,128)}, bf16[3,3,4,256]{3,2,1,0:T(4,128)(2,1)}) custom-call(bf16[64,3072]{1,0:T(8,128)(2,1)} %get-tuple-element.12.qkv_next, bf16[32,2048]{1,0:T(8,128)(2,1)} %get-tuple-element.13.stream_out, bf16[1024,128]{1,0:T(8,128)(2,1)} %get-tuple-element.14.states, ...), custom_call_target="tpu_custom_call" | custom-call | tf_op jit(solution)/shard_map/place_results/pallas_call | solution.py:621
